TPU v7x, 512 devices: a whole 4x4x16 slice. The times are simulated.
512 devices in a mesh: view: 32 (over y, z_lo), eye: 2 (over z_hi), seq: 8 (over x, core).
Axes of the slice: x: 4, y: 4, z: 16 (z_hi: 2, z_lo: 8; z = z_hi * 8 + z_lo), core: 2. Of those that a mesh axis runs over, the one named last changes fastest.
Arguments:
- queries: bfloat16 [32, 2, 1024, 4096], P('view', 'eye', 'seq'), may hold values from -6 to 6
- keys: bfloat16 [32, 2, 1024, 4096], P('view', 'eye', 'seq'), may hold values from -6 to 6
- values: bfloat16 [32, 2, 1024, 4096], P('view', 'eye', 'seq'), may hold values from -60 to 60
- fwd_index: int32 [32, 2, 4, 3072], P('view', 'eye'), may hold values from 0 to 127
- fwd_weight: float32 [32, 2, 4, 3072], P('view', 'eye'), may hold values from 0.1 to 1
- own_map: int32 [32, 2, 2, 1024], P('view', 'eye'), may hold values 0 or 1
- back_index: int32 [32, 2, 4, 1024], P('view', 'eye'), may hold values from 0 to 383
- back_weight: float32 [32, 2, 4, 1024], P('view', 'eye'), may hold values from 0.1 to 1
- head_gain: float32 [4096], replicated, may hold values from 0.1 to 1.9
- head_shift: float32 [4096], replicated, may hold values from -3 to 3
- head_weight: bfloat16 [4096, 64], replicated, may hold values from -0.09375 to 0.09375
- latents: float32 [32, 2, 64, 1024], P('view', 'eye', None, 'seq'), may hold values from -6 to 6
- eye_mix: float32 [64], replicated, may hold values from 0.2 to 0.5
Outputs:
- updated: float32 [32, 2, 64, 1024], P('view', 'eye', None, 'seq')
All inputs are finite; a program needn't handle non-finite values. No bound on the sum of `own_map` on one device may be relied on, other than what follows from the above.
Results may differ from a plain program's by a relative error of at most 0.007.
Values may be sent and summed in bfloat16 or wider, within the bound.
A program may use at most 64 MiB of HBM per device.

v0:
```python
import math

import jax
import jax.numpy as jnp
from jax import lax
from jax.sharding import PartitionSpec as P

DH = 128


def padded(value, sides, width):
    for axis, dim in sides:
        size, length = (lax.axis_size(axis), value.shape[dim])
        up = [(i, (i + 1) % size) for i in range(size)]
        down = [(j, i) for i, j in up]
        last = lax.slice_in_dim(value, length - width, length, axis=dim)
        leading = lax.slice_in_dim(value, 0, width, axis=dim)
        before = lax.ppermute(last, axis, up)
        after = lax.ppermute(leading, axis, down)
        value = jnp.concatenate([before, value, after], axis=dim)
    return value


def partner(value, axis, distance):
    mask = 2**distance
    pairs = [(source, source ^ mask) for source in range(lax.axis_size(axis))]
    return lax.ppermute(value, axis, pairs)


def attend(parts):
    query, keyset, valueset = parts
    length = query.shape[0]
    heads_here = query.shape[2]
    head_size = query.shape[3]
    block = min(512, length)
    scale = 1.0 / math.sqrt(head_size)
    key_rows = keyset[:, 0]
    value_rows = valueset[:, 0]

    def one_block(rows):
        scores = (
            jnp.einsum("qhd,khd->hqk", rows, key_rows, preferred_element_type=jnp.float32) * scale
        )
        highest = jnp.max(scores, axis=2, keepdims=True)
        probs = jnp.exp(scores - highest)
        total = jnp.sum(probs, axis=2)
        mixed = jnp.einsum(
            "hqk,khd->qhd",
            probs.astype(jnp.bfloat16),
            value_rows,
            preferred_element_type=jnp.float32,
        )
        return (mixed / jnp.transpose(total)[:, :, None]).astype(jnp.bfloat16)

    blocks_all = query[:, 0].reshape(length // block, block, heads_here, head_size)
    return lax.map(one_block, blocks_all).reshape(length, 1, heads_here, head_size)


def resample(taps, raw, source):
    columns = source.shape[1]
    norm_taps = raw / jnp.sum(raw, axis=0, keepdims=True)
    positions = lax.broadcasted_iota(jnp.int32, (1, 1, columns), 2)
    matrix = jnp.zeros((taps.shape[1], taps.shape[2], columns), jnp.float32)
    for tap in range(4):
        matrix = matrix + norm_taps[tap][:, :, None] * (taps[tap][:, :, None] == positions).astype(
            jnp.float32
        )
    upper = matrix.astype(jnp.bfloat16)
    lower = (matrix - upper.astype(jnp.float32)).astype(jnp.bfloat16)
    first = jnp.einsum("grc,gcw->grw", upper, source, preferred_element_type=jnp.float32)
    second = jnp.einsum("grc,gcw->grw", lower, source, preferred_element_type=jnp.float32)
    return first + second


def join(groups, fwd_taps, fwd_raw, present_map, back_taps, back_raw):
    count = groups.shape[1]
    contrib = resample(fwd_taps, fwd_raw, groups).astype(jnp.bfloat16)
    widened = padded(contrib, (("view", 1),), count)
    present = present_map.astype(jnp.float32)
    centre = contrib[:, count : 2 * count].astype(jnp.float32)
    from_prev = widened[:, :count].astype(jnp.float32)
    from_next = widened[:, 4 * count :].astype(jnp.float32)
    summed_tile = centre + present[0][:, :, None] * from_prev + present[1][:, :, None] * from_next
    joined = (summed_tile / (1.0 + present[0] + present[1])[:, :, None]).astype(jnp.bfloat16)
    extended = padded(joined, (("view", 1),), count)
    return resample(back_taps, back_raw, extended).astype(jnp.bfloat16)


def whole_tokens(blended, head_gain, head_shift, head_weight):
    widened = blended.astype(jnp.float32)
    centre_mean = jnp.mean(widened, axis=1, keepdims=True)
    centred = widened - centre_mean
    variance = jnp.mean(centred * centred, axis=1, keepdims=True)
    normed = centred / jnp.sqrt(variance + 1e-06) * head_gain + head_shift
    return lax.dot_general(
        head_weight.astype(jnp.float32),
        normed,
        (((0,), (1,)), ((), ())),
        precision=lax.Precision.HIGHEST,
    )


def local(
    queries,
    keys,
    values,
    fwd_index,
    fwd_weight,
    own_map,
    back_index,
    back_weight,
    head_gain,
    head_shift,
    head_weight,
    latents,
    eye_mix,
):
    groups_count = lax.axis_size("seq")
    count = queries.shape[2]
    width = queries.shape[3]
    heads_here = width // DH // groups_count
    split_shape = (count, groups_count, heads_here, DH)
    attended = attend(
        (
            lax.all_to_all(
                queries[0, 0].reshape(split_shape), "seq", split_axis=1, concat_axis=0, tiled=True
            ),
            lax.all_to_all(
                keys[0, 0].reshape(split_shape), "seq", split_axis=1, concat_axis=0, tiled=True
            ),
            lax.all_to_all(
                values[0, 0].reshape(split_shape), "seq", split_axis=1, concat_axis=0, tiled=True
            ),
        )
    )
    gathered = lax.all_to_all(attended, "seq", split_axis=0, concat_axis=1, tiled=True)
    groups = gathered.reshape(1, count, width)
    group = lax.axis_index("seq")
    fwd_taps = lax.dynamic_slice_in_dim(fwd_index[0, 0], group * 3 * count, 3 * count, 1)[
        :, None, :
    ]
    fwd_raw = lax.dynamic_slice_in_dim(fwd_weight[0, 0], group * 3 * count, 3 * count, 1)[
        :, None, :
    ]
    present_map = lax.dynamic_slice_in_dim(own_map[0, 0], group * count, count, 1)[:, None, :]
    back_taps = lax.dynamic_slice_in_dim(back_index[0, 0], group * count, count, 1)[:, None, :]
    back_raw = lax.dynamic_slice_in_dim(back_weight[0, 0], group * count, count, 1)[:, None, :]
    blended = join(groups, fwd_taps, fwd_raw, present_map, back_taps, back_raw)[0]
    velocity = whole_tokens(blended, head_gain, head_shift, head_weight)
    other = partner(velocity.astype(jnp.bfloat16), "eye", 0).astype(velocity.dtype)
    mixed = velocity + eye_mix[:, None] * (other - velocity)
    updated = latents[0, 0] - 0.8 * mixed
    return updated.reshape(1, 1, updated.shape[0], updated.shape[1])


def solution(mesh):
    placed = (
        P("view", "eye", "seq", None),
        P("view", "eye", "seq", None),
        P("view", "eye", "seq", None),
        P("view", "eye", None, None),
        P("view", "eye", None, None),
        P("view", "eye", None, None),
        P("view", "eye", None, None),
        P("view", "eye", None, None),
        P(),
        P(),
        P(),
        P("view", "eye", None, "seq"),
        P(),
    )
    return jax.shard_map(
        local, mesh=mesh, in_specs=placed, out_specs=P("view", "eye", None, "seq"), check_vma=False
    )
```

profile of v0, /device:TPU:32, one launch (start us, length us, event | category | flops | bytes accessed | tf_op | source)
XLA Modules:
  0.0 239.1 jit_solution(15385360355609153394)
XLA Ops:
  0.0 0.0 copy-start
  0.0 2.3 copy.33
  2.3 4.3 %all-to-all-start = ((bf16[128,8,4,128]{0,3,2,1:T(8,128)(2,1)}), bf16[128,8,4,128]{0,3,2,1:T(8,128)(2,1)S(1)}, u32[]{:S(2)}, u32[]{:S(2)}) async-start(bf16[128,8,4,128]{0,3,2,1:T(8,128)(2,1)} %bitcast.17), calls=%async_computation | async-start | bytes 2097152 | tf_op jit(solution)/shard_map/all_to_all | solution.py:125
  6.6 1.6 copy.35
  8.3 1.3 copy.36
  9.6 13.0 %all-to-all-done = bf16[128,8,4,128]{0,3,2,1:T(8,128)(2,1)S(1)} async-done(((bf16[128,8,4,128]{0,3,2,1:T(8,128)(2,1)}), bf16[128,8,4,128]{0,3,2,1:T(8,128)(2,1)S(1)}, u32[]{:S(2)}, u32[]{:S(2)}) %all-to-all-start) | async-done | bytes 1048608 | tf_op jit(solution)/shard_map/all_to_all | solution.py:125
  22.6 3.6 %all-to-all-start.1 = ((bf16[128,8,4,128]{3,0,2,1:T(8,128)(2,1)}), bf16[128,8,4,128]{3,0,2,1:T(8,128)(2,1)S(1)}, u32[]{:S(2)}, u32[]{:S(2)}) async-start(bf16[128,8,4,128]{3,0,2,1:T(8,128)(2,1)} %copy.36), calls=%async_computation.1 | async-start | bytes 2097152 | tf_op jit(solution)/shard_map/all_to_all | solution.py:128
  26.2 2.3 copy.38
  28.5 2.3 copy.39
  30.7 11.3 %all-to-all-done.1 = bf16[128,8,4,128]{3,0,2,1:T(8,128)(2,1)S(1)} async-done(((bf16[128,8,4,128]{3,0,2,1:T(8,128)(2,1)}), bf16[128,8,4,128]{3,0,2,1:T(8,128)(2,1)S(1)}, u32[]{:S(2)}, u32[]{:S(2)}) %all-to-all-start.1) | async-done | bytes 1048608 | tf_op jit(solution)/shard_map/all_to_all | solution.py:128
  42.1 4.2 %all-to-all-start.2 = ((bf16[128,8,4,128]{3,0,2,1:T(8,128)(2,1)}), bf16[128,8,4,128]{3,0,2,1:T(8,128)(2,1)}, u32[]{:S(2)}, u32[]{:S(2)}) async-start(bf16[128,8,4,128]{3,0,2,1:T(8,128)(2,1)} %copy.39), calls=%async_computation.2 | async-start | bytes 2097152 | tf_op jit(solution)/shard_map/all_to_all | solution.py:131
  46.3 0.0 copy-done.2
  46.3 0.7 copy.34
  47.0 1.3 copy.37
  48.3 14.0 %all-to-all-done.2 = bf16[128,8,4,128]{3,0,2,1:T(8,128)(2,1)} async-done(((bf16[128,8,4,128]{3,0,2,1:T(8,128)(2,1)}), bf16[128,8,4,128]{3,0,2,1:T(8,128)(2,1)}, u32[]{:S(2)}, u32[]{:S(2)}) %all-to-all-start.2) | async-done | bytes 1048608 | tf_op jit(solution)/shard_map/all_to_all | solution.py:131
  62.3 2.3 copy.40
  64.6 12.5 %while.10 = (s32[]{:T(128)}, bf16[2,512,4,128]{3,1,0,2:T(8,128)(2,1)}, bf16[2,512,4,128]{3,1,0,2:T(8,128)(2,1)S(1)}, bf16[1024,4,128]{2,0,1:T(8,128)(2,1)S(1)}, bf16[1024,4,128]{2,0,1:T(8,128)(2,1)}, /*index=5*/s32[]{:T(128)}) while((s32[]{:T(128)}, bf16[2,512,4,128]{3,1,0,2:T(8,128)(2,1)}, bf16[2,512,4,128]{3,1,0,2:T(8,128)(2,1)S(1)}, ...), condition=%wide.region_5.6_spmd, body=%wide.region_2.5_spmd.sunk | while | flops 1091039232 | bytes 40935592 | solution.py:56
  64.6 1.3 multiply_reduce_fusion.3
  65.9 0.0 copy-start.4
  66.0 1.9 fusion.98
  67.8 2.0 fusion.99
  69.8 1.0 copy-done.5
  70.9 1.3 multiply_reduce_fusion.3
  72.2 0.0 copy-start.4
  72.2 1.9 fusion.98
  74.1 2.0 fusion.99
  76.1 1.0 copy-done.5
  77.1 3.0 %copy.43 = bf16[1024,1,4,128]{3,2,1,0:T(4,128)(2,1)} copy(bf16[1024,1,4,128]{3,0,2,1:T(8,128)(2,1)} %bitcast.127) | data formatting | bytes 2097152 | tf_op jit(solution)/shard_map/reshape | solution.py:56
  80.2 3.6 %all-to-all-start.3 = ((bf16[1024,1,4,128]{3,2,1,0:T(4,128)(2,1)}), bf16[1024,1,4,128]{3,2,1,0:T(4,128)(2,1)S(1)}, u32[]{:S(2)}, u32[]{:S(2)}) async-start(bf16[1024,1,4,128]{3,2,1,0:T(4,128)(2,1)} %copy.43), calls=%async_computation.3 | async-start | bytes 2097152 | tf_op jit(solution)/shard_map/all_to_all | solution.py:136
  83.7 0.7 dynamic-slice_reduce_fusion
  84.4 0.9 fusion.71
  85.4 0.7 bitcast_divide_fusion
  86.1 13.5 %all-to-all-done.3 = bf16[1024,1,4,128]{3,2,1,0:T(4,128)(2,1)S(1)} async-done(((bf16[1024,1,4,128]{3,2,1,0:T(4,128)(2,1)}), bf16[1024,1,4,128]{3,2,1,0:T(4,128)(2,1)S(1)}, u32[]{:S(2)}, u32[]{:S(2)}) %all-to-all-start.3) | async-done | bytes 1048608 | tf_op jit(solution)/shard_map/all_to_all | solution.py:136
  99.6 0.1 copy.44
  99.8 0.7 copy.45
  100.4 1.8 fusion.44
  102.2 1.6 fusion.22
  103.8 0.0 copy-start.1
  103.8 1.7 copy-done.1
  105.5 1.5 fusion.82
  107.0 6.6 %collective-permute-start.1 = (bf16[1,128,4096]{2,1,0:T(8,128)(2,1)}, bf16[1,128,4096]{2,1,0:T(8,128)(2,1)S(1)}, u32[]{:S(2)}, u32[]{:S(2)}) collective-permute-start(bf16[1,128,4096]{2,1,0:T(8,128)(2,1)} %get-tuple-element.76), channel_id=1, source_target_pairs={{16,0},{32,16},{48,32},{64,48},{80,64},{96,80},{112,96},{128,112},... | collective-permute-start | bytes 3145736 | tf_op jit(solution)/shard_map/ppermute | solution.py:19
  113.6 1.9 collective-permute-start
  115.5 0.7 fusion.74
  116.2 19.8 %collective-permute-done.1 = bf16[1,128,4096]{2,1,0:T(8,128)(2,1)S(1)} collective-permute-done((bf16[1,128,4096]{2,1,0:T(8,128)(2,1)}, bf16[1,128,4096]{2,1,0:T(8,128)(2,1)S(1)}, u32[]{:S(2)}, u32[]{:S(2)}) %collective-permute-start.1) | collective-permute-done | bytes 1048608 | tf_op jit(solution)/shard_map/ppermute | solution.py:19
  136.1 32.0 %collective-permute-done = bf16[1,128,4096]{2,1,0:T(8,128)(2,1)S(1)} collective-permute-done((bf16[1,128,4096]{2,1,0:T(8,128)(2,1)}, bf16[1,128,4096]{2,1,0:T(8,128)(2,1)S(1)}, u32[]{:S(2)}, u32[]{:S(2)}) %collective-permute-start) | collective-permute-done | bytes 1048608 | tf_op jit(solution)/shard_map/ppermute | solution.py:18
  168.1 2.0 divide_convert_fusion.1
  170.2 2.2 collective-permute-start.3
  172.3 3.9 %collective-permute-start.2 = (bf16[1,128,4096]{2,1,0:T(8,128)(2,1)S(1)}, bf16[1,128,4096]{2,1,0:T(8,128)(2,1)S(1)}, u32[]{:S(2)}, u32[]{:S(2)}) collective-permute-start(bf16[1,128,4096]{2,1,0:T(8,128)(2,1)S(1)} %divide_convert_fusion.1), channel_id=1, source_target_pairs={{0,16},{16,32},{32,48},{48,64},{64,80},{80,96},{96,112},{112,128},... | collective-permute-start | bytes 3145736 | tf_op jit(solution)/shard_map/ppermute | solution.py:18
  176.2 0.7 fusion.81
  176.9 0.7 constant_dynamic-slice_fusion.6
  177.6 40.7 %collective-permute-done.3 = bf16[1,128,4096]{2,1,0:T(8,128)(2,1)S(1)} collective-permute-done((bf16[1,128,4096]{2,1,0:T(8,128)(2,1)S(1)}, bf16[1,128,4096]{2,1,0:T(8,128)(2,1)S(1)}, u32[]{:S(2)}, u32[]{:S(2)}) %collective-permute-start.3) | collective-permute-done | bytes 1048608 | tf_op jit(solution)/shard_map/ppermute | solution.py:19
  218.4 1.8 collective-permute-done.2
  220.1 0.8 fusion.30
  221.0 0.0 copy-start.8
  221.0 0.0 copy-start.9
  221.0 1.0 fusion.83
  222.0 0.4 multiply_reduce_fusion.1
  222.4 0.0 copy-start.6
  222.4 0.0 copy-start.7
  222.4 1.7 fusion.84
  224.1 8.8 %collective-permute-start.4 = (bf16[64,128]{1,0:T(8,128)(2,1)S(1)}, bf16[64,128]{1,0:T(8,128)(2,1)S(1)}, u32[]{:S(2)}, u32[]{:S(2)}) collective-permute-start(bf16[64,128]{1,0:T(8,128)(2,1)S(1)} %get-tuple-element.89), channel_id=1, source_target_pairs={{0,8},{8,0},{1,9},{9,1},{2,10},{10,2},{3,11},{11,3},{4,12},{12,4},... | collective-permute-start | bytes 49160 | tf_op jit(solution)/shard_map/ppermute | solution.py:27
  232.8 5.6 %collective-permute-done.4 = bf16[64,128]{1,0:T(8,128)(2,1)S(1)} collective-permute-done((bf16[64,128]{1,0:T(8,128)(2,1)S(1)}, bf16[64,128]{1,0:T(8,128)(2,1)S(1)}, u32[]{:S(2)}, u32[]{:S(2)}) %collective-permute-start.4) | collective-permute-done | bytes 16416 | tf_op jit(solution)/shard_map/ppermute | solution.py:27
  238.4 0.0 copy-done.6
  238.4 0.7 fusion.69
  (22 shorter events, 0.1 us)
Async XLA Ops:
  0.0 222.4 %copy-start = (bf16[4096,64]{0,1:T(8,128)(2,1)S(1)}, bf16[4096,64]{0,1:T(8,128)(2,1)}, u32[]{:S(2)}) copy-start(bf16[4096,64]{0,1:T(8,128)(2,1)} %param.25) | copy-start | bytes 1572868
  2.3 20.3 %all-to-all-start = ((bf16[128,8,4,128]{0,3,2,1:T(8,128)(2,1)}), bf16[128,8,4,128]{0,3,2,1:T(8,128)(2,1)S(1)}, u32[]{:S(2)}, u32[]{:S(2)}) async-start(bf16[128,8,4,128]{0,3,2,1:T(8,128)(2,1)} %bitcast.17), calls=%async_computation | async-start | bytes 2097152 | tf_op jit(solution)/shard_map/all_to_all | solution.py:125
  22.6 19.4 %all-to-all-start.1 = ((bf16[128,8,4,128]{3,0,2,1:T(8,128)(2,1)}), bf16[128,8,4,128]{3,0,2,1:T(8,128)(2,1)S(1)}, u32[]{:S(2)}, u32[]{:S(2)}) async-start(bf16[128,8,4,128]{3,0,2,1:T(8,128)(2,1)} %copy.36), calls=%async_computation.1 | async-start | bytes 2097152 | tf_op jit(solution)/shard_map/all_to_all | solution.py:128
  42.1 4.3 %copy-start.2 = (bf16[128,8,4,128]{3,0,2,1:T(8,128)(2,1)}, bf16[128,8,4,128]{3,0,2,1:T(8,128)(2,1)S(1)}, u32[]{:S(2)}) copy-start(bf16[128,8,4,128]{3,0,2,1:T(8,128)(2,1)S(1)} %all-to-all-done.1) | copy-start | bytes 3145732
  42.1 20.2 %all-to-all-start.2 = ((bf16[128,8,4,128]{3,0,2,1:T(8,128)(2,1)}), bf16[128,8,4,128]{3,0,2,1:T(8,128)(2,1)}, u32[]{:S(2)}, u32[]{:S(2)}) async-start(bf16[128,8,4,128]{3,0,2,1:T(8,128)(2,1)} %copy.39), calls=%async_computation.2 | async-start | bytes 2097152 | tf_op jit(solution)/shard_map/all_to_all | solution.py:131
  65.9 1.9 copy-start.3
  65.9 1.9 copy-start.4
  69.8 1.0 copy-start.5
  72.2 1.9 copy-start.3
  72.2 1.9 copy-start.4
  76.1 1.0 copy-start.5
  80.2 19.4 %all-to-all-start.3 = ((bf16[1024,1,4,128]{3,2,1,0:T(4,128)(2,1)}), bf16[1024,1,4,128]{3,2,1,0:T(4,128)(2,1)S(1)}, u32[]{:S(2)}, u32[]{:S(2)}) async-start(bf16[1024,1,4,128]{3,2,1,0:T(4,128)(2,1)} %copy.43), calls=%async_computation.3 | async-start | bytes 2097152 | tf_op jit(solution)/shard_map/all_to_all | solution.py:136
  103.8 1.7 copy-start.1
  107.0 29.1 %collective-permute-start.1 = (bf16[1,128,4096]{2,1,0:T(8,128)(2,1)}, bf16[1,128,4096]{2,1,0:T(8,128)(2,1)S(1)}, u32[]{:S(2)}, u32[]{:S(2)}) collective-permute-start(bf16[1,128,4096]{2,1,0:T(8,128)(2,1)} %get-tuple-element.76), channel_id=1, source_target_pairs={{16,0},{32,16},{48,32},{64,48},{80,64},{96,80},{112,96},{128,112},... | collective-permute-start | bytes 3145736 | tf_op jit(solution)/shard_map/ppermute | solution.py:19
  113.6 54.5 %collective-permute-start = (bf16[1,128,4096]{2,1,0:T(8,128)(2,1)}, bf16[1,128,4096]{2,1,0:T(8,128)(2,1)S(1)}, u32[]{:S(2)}, u32[]{:S(2)}) collective-permute-start(bf16[1,128,4096]{2,1,0:T(8,128)(2,1)} %get-tuple-element.75), channel_id=1, source_target_pairs={{0,16},{16,32},{32,48},{48,64},{64,80},{80,96},{96,112},{112,128},... | collective-permute-start | bytes 3145736 | tf_op jit(solution)/shard_map/ppermute | solution.py:18
  170.2 48.2 %collective-permute-start.3 = (bf16[1,128,4096]{2,1,0:T(8,128)(2,1)S(1)}, bf16[1,128,4096]{2,1,0:T(8,128)(2,1)S(1)}, u32[]{:S(2)}, u32[]{:S(2)}) collective-permute-start(bf16[1,128,4096]{2,1,0:T(8,128)(2,1)S(1)} %divide_convert_fusion.1), channel_id=1, source_target_pairs={{16,0},{32,16},{48,32},{64,48},{80,64},{96,80},{112,96},{128,112},... | collective-permute-start | bytes 3145736 | tf_op jit(solution)/shard_map/ppermute | solution.py:19
  172.3 47.8 %collective-permute-start.2 = (bf16[1,128,4096]{2,1,0:T(8,128)(2,1)S(1)}, bf16[1,128,4096]{2,1,0:T(8,128)(2,1)S(1)}, u32[]{:S(2)}, u32[]{:S(2)}) collective-permute-start(bf16[1,128,4096]{2,1,0:T(8,128)(2,1)S(1)} %divide_convert_fusion.1), channel_id=1, source_target_pairs={{0,16},{16,32},{32,48},{48,64},{64,80},{80,96},{96,112},{112,128},... | collective-permute-start | bytes 3145736 | tf_op jit(solution)/shard_map/ppermute | solution.py:18
  221.0 1.4 copy-start.8
  221.0 1.4 copy-start.9
  222.4 16.0 %copy-start.6 = (f32[1,1,64,128]{3,2,1,0:T(8,128)S(1)}, f32[1,1,64,128]{3,2,1,0:T(8,128)}, u32[]{:S(2)}) copy-start(f32[1,1,64,128]{3,2,1,0:T(8,128)} %param.26) | copy-start | bytes 98308
  222.4 16.0 %copy-start.7 = (f32[64]{0:T(128)S(1)}, f32[64]{0:T(128)}, u32[]{:S(2)}) copy-start(f32[64]{0:T(128)} %param.27) | copy-start | bytes 772
  224.1 14.3 %collective-permute-start.4 = (bf16[64,128]{1,0:T(8,128)(2,1)S(1)}, bf16[64,128]{1,0:T(8,128)(2,1)S(1)}, u32[]{:S(2)}, u32[]{:S(2)}) collective-permute-start(bf16[64,128]{1,0:T(8,128)(2,1)S(1)} %get-tuple-element.89), channel_id=1, source_target_pairs={{0,8},{8,0},{1,9},{9,1},{2,10},{10,2},{3,11},{11,3},{4,12},{12,4},... | collective-permute-start | bytes 49160 | tf_op jit(solution)/shard_map/ppermute | solution.py:27
where the time goes:
time: 240 us; the launch traced here: 239 us
  waiting for transfers between devices  152 us (63%)
  starting transfers between devices  39 us (16%)
  local copies, waits for them, and re-layouts  24.9 us (10%)
  matrix products  13.5 us (6%)
  other arithmetic  9.68 us (4%)
    ppermute x2, waiting for transfers between devices, padded(): after = lax.ppermute(leading, axis, down)  60.6 us
    ppermute x2, waiting for transfers between devices, padded(): before = lax.ppermute(last, axis, up)  33.8 us
    all_to_all x1, waiting for transfers between devices, local(): lax.all_to_all(values[0, 0].reshape(split_shape), 'seq', split_axis=1, co...  14 us
    all_to_all x1, waiting for transfers between devices, local(): lax.all_to_all(attended, 'seq', split_axis=0, concat_axis=1, tiled=True)  13.5 us
    all_to_all x1, waiting for transfers between devices, local(): lax.all_to_all(queries[0, 0].reshape(split_shape), 'seq', split_axis=1, c...  13 us
    all_to_all x1, waiting for transfers between devices, local(): lax.all_to_all(keys[0, 0].reshape(split_shape), 'seq', split_axis=1, conc...  11.3 us
    ppermute x1, starting transfers between devices, partner(): return lax.ppermute(value, axis, pairs)  8.76 us
    ppermute x2, starting transfers between devices, padded(): after = lax.ppermute(leading, axis, down)  8.75 us
  transfers between devices with their start and end apart: 9, of which 9 were waited for; matrix products, arithmetic and copies ran while one was open for 6% of the time, Pallas kernels for 0%

commit v1 on v0

v1 whole, which is shorter than its diff:
```python
import math

import jax
import jax.numpy as jnp
from jax import lax
from jax.experimental import pallas as pl
from jax.experimental.pallas import tpu as pltpu
from jax.sharding import PartitionSpec as P

DH = 128
TOK = 128
SEQ = 8
ROW = 8
HERE = 4
FEAT = HERE * DH
LAT = 64
PACK = 40
MESH = pl.DeviceIdType.MESH
BF = jnp.bfloat16
F32 = jnp.float32


def dot(a, b, dims):
    return lax.dot_general(a, b, (dims, ((), ())), preferred_element_type=F32)


def split(x):
    upper = x.astype(BF)
    return upper, (x - upper.astype(F32)).astype(BF)


def wait(ref, sem):
    pltpu.make_async_copy(ref, ref, sem).wait()


def spread(index, weight, rows):
    places = lax.broadcasted_iota(jnp.int32, (rows, TOK), 0).astype(F32)
    total = jnp.zeros((rows, TOK), F32)
    for tap in range(4):
        total = total + jnp.where(places == index[tap : tap + 1], weight[tap : tap + 1], 0.0)
    return total


def kernel(
    q, k, v, fi_in, fw_in, om_in, bi_in, bw_in, gain_in, shift_in, hw_in, lat_in, mix_in, out,
    fi, fw, om, bi, bw, gain, shift, hw, lat, mix,
    kb, vb, qb, att, ext, pks, pk, vt, jt, mt, acc, stats, wg, gsum, hsum, cols, sp, rp, vs, vsb, vown, voth,
    ins, xs, xr, zs, zr, ys, yr, ps, pr, pys, pyr, rs, rr, fs, fr,
):
    view, eye, seq = lax.axis_index("view"), lax.axis_index("eye"), lax.axis_index("seq")
    row, z = view // ROW, view % ROW
    first = row * ROW
    edge = (z + 2) // 4
    nxt, prv = (view + ROW) % 32, (view + 32 - ROW) % 32
    partner = {"view": first + seq, "eye": eye, "seq": z}
    across = {"view": first + seq, "eye": 1 - eye, "seq": z}

    def along_seq(i):
        return {"view": view, "eye": eye, "seq": i}

    def along_view(i):
        return {"view": i, "eye": eye, "seq": seq}

    def send(src, dst, s, r, target):
        pltpu.make_async_remote_copy(
            src_ref=src, dst_ref=dst, send_sem=s, recv_sem=r, device_id=target, device_id_type=MESH
        ).start()

    def copy(src, dst, s):
        pltpu.make_async_copy(src, dst, s).start()

    small = (
        (fi_in, fi), (fw_in, fw), (om_in, om), (bi_in, bi), (bw_in, bw),
        (gain_in, gain), (shift_in, shift), (hw_in, hw), (lat_in, lat), (mix_in, mix),
    )
    for i, (src, dst) in enumerate(small):
        copy(src, dst, ins.at[i])

    barrier = pltpu.get_barrier_semaphore()

    def greet(target):
        pl.semaphore_signal(barrier, inc=1, device_id=target, device_id_type=MESH)

    for step in range(1, SEQ):
        greet(along_seq((seq + step) % SEQ))
        greet(along_view(first + (z + step) % ROW))
    greet(along_view(nxt))
    greet(along_view(prv))
    greet(across)

    @pl.when(z != seq)
    def _():
        greet(partner)

    pl.semaphore_wait(barrier, 2 * (SEQ - 1) + 3 + jnp.where(z == seq, 0, 1))

    arrays = ((k, kb), (v, vb), (q, qb))

    def send_head(h, core):
        for t, (src, dst) in enumerate(arrays):

            def one(step, _):
                other = (seq // 2 + step) % 4 * 2 + core
                start = pl.multiple_of((other * HERE + h) * DH, DH)
                block = src.at[0, 0, :, pl.ds(start, DH)]

                @pl.when(other != seq)
                def _():
                    send(block, dst.at[h, seq], xs.at[t, h], xr.at[t, h], along_seq(other))

                @pl.when(other == seq)
                def _():
                    copy(block, dst.at[h, seq], xr.at[t, h])

                return 0

            lax.fori_loop(0, 4, one, 0)

    send_head(0, 0)
    send_head(0, 1)

    for i, (src, dst) in enumerate(small):
        pltpu.make_async_copy(src, dst, ins.at[i]).wait()

    fwd_raw, back_raw = fw[0, 0], bw[0, 0]
    fwd_norm = fwd_raw / jnp.sum(fwd_raw, axis=0, keepdims=True)
    back_norm = back_raw / jnp.sum(back_raw, axis=0, keepdims=True)
    fwd_place, back_place = fi[0, 0].astype(F32), bi[0, 0].astype(F32)
    present = om[0, 0].astype(F32)
    for g in range(SEQ):
        for tile in range(3):
            at = (g * 3 + tile) * TOK
            pks[g, tile * 4 : tile * 4 + 4, :] = fwd_place[:, at : at + TOK]
            pks[g, 12 + tile * 4 : 16 + tile * 4, :] = fwd_norm[:, at : at + TOK]
        at = g * TOK
        pks[g, 24:28, :] = back_place[:, at : at + TOK]
        pks[g, 28:32, :] = back_norm[:, at : at + TOK]
        pks[g, 32:34, :] = present[:, at : at + TOK]
        pks[g, 34:40, :] = jnp.zeros((6, TOK), F32)
    copy(pks.at[z], pk.at[2 + z], pr.at[edge])

    def send_pack(step, _):
        other = (z + step) % ROW
        send(pks.at[other], pk.at[2 + z], ps, pr.at[edge], along_view(first + other))
        return 0

    lax.fori_loop(1, ROW, send_pack, 0)

    for h in range(1, HERE):
        send_head(h, 0)
        send_head(h, 1)

    def head_sums(c, carry):
        at = pl.multiple_of(c * FEAT, FEAT)
        turned = hw[:, pl.ds(at, FEAT)].astype(F32)
        gained = jnp.sum(turned * gain[:, pl.ds(at, FEAT)], axis=1, keepdims=True)
        gsum[c] = jnp.broadcast_to(gained, (LAT, TOK))
        return carry + jnp.sum(turned * shift[:, pl.ds(at, FEAT)], axis=1, keepdims=True)

    shift_sum = lax.fori_loop(0, SEQ, head_sums, jnp.zeros((LAT, 1), F32))
    for h in range(HERE):
        at = pl.multiple_of((seq * HERE + h) * DH, DH)
        scaled = hw[:, pl.ds(at, DH)].astype(F32) * gain[:, pl.ds(at, DH)]
        wg[h] = jnp.concatenate(split(scaled), axis=0)
        hsum[h] = jnp.broadcast_to(jnp.sum(scaled, axis=1, keepdims=True), (LAT, TOK))
    diagonal = lax.broadcasted_iota(jnp.int32, (LAT, LAT), 0) == lax.broadcasted_iota(
        jnp.int32, (LAT, LAT), 1
    )
    mix_col = jnp.sum(
        jnp.where(diagonal, jnp.broadcast_to(mix[...], (LAT, LAT)), 0.0), axis=1, keepdims=True
    )
    cols[0] = jnp.broadcast_to(shift_sum, (LAT, TOK))
    cols[1] = jnp.broadcast_to(mix_col, (LAT, TOK))

    rate = math.log2(math.e) / math.sqrt(DH)

    def attend(h):
        for t, (_, dst) in enumerate(arrays):
            wait(dst.at[h], xr.at[t, h])

        vt[...] = vb[h].reshape(SEQ * TOK, DH).T

        def block(step, _):
            j = (step + 2 * (1 - z // 4)) % 4
            rows = qb[h, pl.ds(2 * j, 2)].reshape(2 * TOK, DH)
            scores = dot(kb[h].reshape(SEQ * TOK, DH), rows, ((1,), (1,)))
            highest = jnp.max(scores, axis=0, keepdims=True)
            probs = jnp.exp2((scores - highest) * rate)
            total = jnp.sum(probs, axis=0, keepdims=True)
            mixed = dot(vt[...], probs.astype(BF), ((1,), (0,)))
            mixed = (mixed / total).astype(BF)
            for half in range(2):
                g = 2 * j + half
                att[h, g] = mixed[:, half * TOK : (half + 1) * TOK]

                @pl.when(g != z)
                def _():
                    send(att.at[h, g], ext.at[h, 2 + z], zs.at[h], zr.at[h, edge], along_view(first + g))

                @pl.when(g == z)
                def _():
                    copy(att.at[h, g], ext.at[h, 2 + z], zr.at[h, edge])

            return 0

        lax.fori_loop(0, SEQ // 2, block, 0)

    def join(u, _):
        a0, a1 = pk[u + 1, 32:33, :], pk[u + 1, 33:34, :]
        share = 1.0 / (1.0 + a0 + a1)
        for i, factor in enumerate((a0 * share, share, a1 * share)):
            tile = 2 - i
            part = spread(
                pk[u + i, tile * 4 : tile * 4 + 4, :],
                pk[u + i, 12 + tile * 4 : 16 + tile * 4, :] * factor,
                TOK,
            )
            upper, lower = split(part)
            jt[u, i * TOK : (i + 1) * TOK, :] = upper
            jt[u, (3 + i) * TOK : (4 + i) * TOK, :] = lower
        return 0


    def compose(w, _):
        back = spread(pk[w + 2, 24:28, :], pk[w + 2, 28:32, :], 3 * TOK)
        parts = [jnp.zeros((TOK, TOK), F32) for _ in range(5)]
        for b in range(3):
            upper, lower = split(back[b * TOK : (b + 1) * TOK])
            wide = dot(jt[w + b], jnp.concatenate([upper, lower], axis=1), ((1,), (0,)))
            wide = wide[:, :TOK] + wide[:, TOK:]
            wide = wide[: 3 * TOK] + wide[3 * TOK :]
            for i in range(3):
                parts[b + i] = parts[b + i] + wide[i * TOK : (i + 1) * TOK]
        for i in range(5):
            upper, lower = split(parts[i])
            mt[w, i * TOK : (i + 1) * TOK, :TOK] = upper
            mt[w, i * TOK : (i + 1) * TOK, TOK:] = lower
        return 0

    attend(0)

    wait(pk.at[2:4], pr.at[0])
    wait(pk.at[8:10], pr.at[2])
    send(pk.at[8:10], pk.at[0:2], pys.at[0], pyr.at[0], along_view(nxt))
    send(pk.at[2:4], pk.at[10:12], pys.at[1], pyr.at[1], along_view(prv))

    attend(1)
    wait(pk.at[4:8], pr.at[1])
    wait(pk.at[0:2], pyr.at[0])
    wait(pk.at[10:12], pyr.at[1])
    lax.fori_loop(0, ROW + 2, join, 0)
    attend(2)
    lax.fori_loop(0, ROW, compose, 0)
    attend(3)

    def blend(h, low, high):
        def one(w, _):
            source = jnp.concatenate([ext[h, w + i] for i in range(5)], axis=1)
            wide = dot(source, mt[w], ((1,), (0,)))
            x = wide[:, :TOK] + wide[:, TOK:]
            mean = jnp.sum(x, axis=0, keepdims=True) * (1.0 / DH)
            centred = x - mean
            stats[w, h : h + 1, :] = mean
            stats[w, HERE + h : HERE + h + 1, :] = jnp.sum(centred * centred, axis=0, keepdims=True)
            wide = dot(wg[h], centred.astype(BF), ((1,), (0,)))
            part = wide[:LAT] + wide[LAT:]
            if h > 0:
                part = part + acc[w]
            if h < HERE - 1:
                acc[w] = part
                return 0

            means = stats[w, 0:HERE, :]
            mean = jnp.sum(means, axis=0, keepdims=True) * (1.0 / HERE)
            apart = means - mean
            squares = jnp.sum(stats[w, HERE:, :] + DH * apart * apart, axis=0, keepdims=True)
            for i in range(HERE):
                part = part + hsum[i] * apart[i : i + 1]
            rows = []
            for row in (mean, squares):
                for _ in range(3):
                    piece = row.astype(BF).astype(F32)
                    rows.append(piece)
                    row = row - piece
            rows.append(jnp.zeros((10, TOK), F32))
            sp[w, 0:LAT, :] = part.astype(BF)
            sp[w, LAT:, :] = jnp.concatenate(rows, axis=0).astype(BF)

            @pl.when(w != seq)
            def _():
                send(sp.at[w], rp.at[seq], rs, rr, along_seq(w))

            @pl.when(w == seq)
            def _():
                copy(sp.at[w], rp.at[seq], rr)

            return 0

        lax.fori_loop(low, high, one, 0)

    for h in range(HERE):
        wait(ext.at[h, 2:4], zr.at[h, 0])
        wait(ext.at[h, 8:10], zr.at[h, 2])
        send(ext.at[h, 8:10], ext.at[h, 0:2], ys.at[h, 0], yr.at[h, 0], along_view(nxt))
        send(ext.at[h, 2:4], ext.at[h, 10:12], ys.at[h, 1], yr.at[h, 1], along_view(prv))
        wait(ext.at[h, 4:8], zr.at[h, 1])
        blend(h, 2, 6)
        wait(ext.at[h, 0:2], yr.at[h, 0])
        blend(h, 0, 2)
        wait(ext.at[h, 10:12], yr.at[h, 1])
        blend(h, 6, 8)

    wait(rp, rr)
    pieces = rp[:, LAT:, :].astype(F32)
    means = pieces[:, 0] + pieces[:, 1] + pieces[:, 2]
    squares = pieces[:, 3] + pieces[:, 4] + pieces[:, 5]
    mean = jnp.sum(means, axis=0, keepdims=True) * (1.0 / SEQ)
    apart = means - mean
    squares = jnp.sum(squares + FEAT * apart * apart, axis=0, keepdims=True)
    deviation = jnp.sqrt(squares * (1.0 / (SEQ * FEAT)) + 1e-06)
    summed = jnp.zeros((LAT, TOK), F32)
    for i in range(SEQ):
        summed = summed + (rp[i, :LAT, :].astype(F32) + gsum[i] * apart[i : i + 1])
    velocity = summed / deviation + cols[0]
    vs[...] = velocity
    vsb[...] = velocity.astype(BF)
    send(vsb, voth, fs.at[1], fr.at[1], across)

    @pl.when(z != seq)
    def _():
        send(vs, vown, fs.at[0], fr.at[0], partner)

    @pl.when(z == seq)
    def _():
        copy(vs, vown, fr.at[0])

    wait(vown, fr.at[0])
    wait(voth, fr.at[1])
    mine = vown[...]
    out[0, 0] = lat[0, 0] - 0.8 * (mine + cols[1] * (voth[...].astype(F32) - mine))

    for h in range(HERE):
        for t, (_, dst) in enumerate(arrays):
            wait(dst.at[h, 0 : SEQ - 1], xs.at[t, h])
        wait(att.at[h, 0 : ROW - 1], zs.at[h])
        wait(ext.at[h, 8:10], ys.at[h, 0])
        wait(ext.at[h, 2:4], ys.at[h, 1])
    wait(pks.at[0 : ROW - 1], ps)
    wait(pk.at[8:10], pys.at[0])
    wait(pk.at[2:4], pys.at[1])
    wait(sp.at[0 : SEQ - 1], rs)
    wait(vsb, fs.at[1])

    @pl.when(z != seq)
    def _():
        wait(vs, fs.at[0])


def local(
    queries, keys, values, fwd_index, fwd_weight, own_map, back_index, back_weight,
    head_gain, head_shift, head_weight, latents, eye_mix,
):
    hbm = pl.BlockSpec(memory_space=pltpu.HBM)
    vmem = pl.BlockSpec(memory_space=pltpu.VMEM)
    dma = pltpu.SemaphoreType.DMA
    block = (TOK, DH)
    return pl.pallas_call(
        kernel,
        out_shape=jax.ShapeDtypeStruct((1, 1, LAT, TOK), F32),
        in_specs=[hbm] * 13,
        out_specs=vmem,
        scratch_shapes=[
            pltpu.VMEM(fwd_index.shape, jnp.int32),
            pltpu.VMEM(fwd_weight.shape, F32),
            pltpu.VMEM(own_map.shape, jnp.int32),
            pltpu.VMEM(back_index.shape, jnp.int32),
            pltpu.VMEM(back_weight.shape, F32),
            pltpu.VMEM((1, SEQ * FEAT), F32),
            pltpu.VMEM((1, SEQ * FEAT), F32),
            pltpu.VMEM((LAT, SEQ * FEAT), BF),
            pltpu.VMEM((1, 1, LAT, TOK), F32),
            pltpu.VMEM((1, LAT), F32),
            pltpu.VMEM((HERE, SEQ) + block, BF),
            pltpu.VMEM((HERE, SEQ) + block, BF),
            pltpu.VMEM((HERE, SEQ) + block, BF),
            pltpu.VMEM((HERE, SEQ) + block, BF),
            pltpu.VMEM((HERE, ROW + 4) + block, BF),
            pltpu.VMEM((SEQ, PACK, TOK), F32),
            pltpu.VMEM((ROW + 4, PACK, TOK), F32),
            pltpu.VMEM((DH, SEQ * TOK), BF),
            pltpu.VMEM((ROW + 2, 6 * TOK, TOK), BF),
            pltpu.VMEM((ROW, 5 * TOK, 2 * TOK), BF),
            pltpu.VMEM((ROW, LAT, TOK), F32),
            pltpu.VMEM((ROW, 2 * HERE, TOK), F32),
            pltpu.VMEM((HERE, 2 * LAT, DH), BF),
            pltpu.VMEM((SEQ, LAT, TOK), F32),
            pltpu.VMEM((HERE, LAT, TOK), F32),
            pltpu.VMEM((2, LAT, TOK), F32),
            pltpu.VMEM((ROW, LAT + 16, TOK), BF),
            pltpu.VMEM((SEQ, LAT + 16, TOK), BF),
            pltpu.VMEM((LAT, TOK), F32),
            pltpu.VMEM((LAT, TOK), BF),
            pltpu.VMEM((LAT, TOK), F32),
            pltpu.VMEM((LAT, TOK), BF),
            dma((10,)),
            dma((3, HERE)), dma((3, HERE)),
            dma((HERE,)), dma((HERE, 3)),
            dma((HERE, 2)), dma((HERE, 2)),
            dma(()), dma((3,)),
            dma((2,)), dma((2,)),
            dma(()), dma(()),
            dma((2,)), dma((2,)),
        ],
        compiler_params=pltpu.CompilerParams(
            collective_id=0, has_side_effects=True, vmem_limit_bytes=60 * 2**20
        ),
    )(
        queries, keys, values, fwd_index, fwd_weight, own_map, back_index, back_weight,
        head_gain.reshape(1, -1), head_shift.reshape(1, -1), head_weight.T, latents,
        eye_mix.reshape(1, -1),
    )


def solution(mesh):
    placed = (
        P("view", "eye", "seq", None),
        P("view", "eye", "seq", None),
        P("view", "eye", "seq", None),
        P("view", "eye", None, None),
        P("view", "eye", None, None),
        P("view", "eye", None, None),
        P("view", "eye", None, None),
        P("view", "eye", None, None),
        P(),
        P(),
        P(),
        P("view", "eye", None, "seq"),
        P(),
    )
    return jax.shard_map(
        local, mesh=mesh, in_specs=placed, out_specs=P("view", "eye", None, "seq"), check_vma=False
    )
```

time: 240 us -> 90.4 us (0.38)
  the two profiles are of different devices: /device:TPU:32 before, /device:TPU:7 now
where the time goes in v1:
time: 90.4 us; the launch traced here: 90.2 us
  Pallas kernels  88.8 us (98%)
  local copies, waits for them, and re-layouts  1.38 us (2%)
    pallas_call x1, Pallas kernels, local(): pl.pallas_call(kernel, out_shape=jax.ShapeDtypeStruct((1, 1, LAT, TOK), F...  88.8 us

profile of v1, /device:TPU:7, one launch (start us, length us, event | category | flops | bytes accessed | tf_op | source)
XLA Modules:
  0.0 90.2 jit_solution(8568856577674450803)
XLA Ops:
  0.0 88.8 %shard_map.127 = f32[1,1,64,128]{3,2,1,0:T(8,128)} custom-call(bf16[1,1,128,4096]{3,2,1,0:T(8,128)(2,1)} %q.1, bf16[1,1,128,4096]{3,2,1,0:T(8,128)(2,1)} %k.1, bf16[1,1,128,4096]{3,2,1,0:T(8,128)(2,1)} %v.1, s32[1,1,4,3072]{3,2,1,0:T(4,128)} %fi_in.1, f32[1,1,4,3072]{3,2,1,0:T(4,128)} %fw_in.1, s32[1,1,2,1024]{3,2,1,0:T(2,128)} %om_in.1, ...), custom_call_target="tpu_custom_call" | custom-call | tf_op jit(solution)/shard_map/pallas_call | solution.py:367
  88.8 1.4 %copy.15 = f32[1,1,64,128]{3,2,1,0:T(8,128)} copy(f32[1,1,64,128]{3,2,1,0:T(8,128)} %shard_map.127) | data formatting | bytes 65536

commit v2 on v1

--- a/solution.py
+++ b/solution.py
@@ -44,8 +44,8 @@
 def kernel(
     q, k, v, fi_in, fw_in, om_in, bi_in, bw_in, gain_in, shift_in, hw_in, lat_in, mix_in, out,
     fi, fw, om, bi, bw, gain, shift, hw, lat, mix,
-    kb, vb, qb, att, ext, pks, pk, vt, jt, mt, acc, stats, wg, gsum, hsum, cols, sp, rp, vs, vsb, vown, voth,
-    ins, xs, xr, zs, zr, ys, yr, ps, pr, pys, pyr, rs, rr, fs, fr,
+    kb, vb, qb, rb, att, ext, pks, pk, vt, jt, mt, acc, stats, wg, gsum, hsum, cols, sp, rp, vs, vsb, vown, voth,
+    ins, xs, xr, bs, br, zs, zr, ys, yr, ps, pr, pys, pyr, rs, rr, fs, fr,
 ):
     view, eye, seq = lax.axis_index("view"), lax.axis_index("eye"), lax.axis_index("seq")
     row, z = view // ROW, view % ROW
@@ -94,30 +94,61 @@
 
     pl.semaphore_wait(barrier, 2 * (SEQ - 1) + 3 + jnp.where(z == seq, 0, 1))
 
+    chip, core = seq // 2, seq % 2
+    opposite = (chip + 2) % 4 * 2
+    target = (chip + 1 + 2 * core) % 4 * 2
+    origin = (chip + 3 - 2 * core) % 4 * 2 + core
     arrays = ((k, kb), (v, vb), (q, qb))
 
-    def send_head(h, core):
-        for t, (src, dst) in enumerate(arrays):
+    def block(src, other, h):
+        start = pl.multiple_of((other * HERE + h) * DH, DH)
+        return src.at[0, 0, :, pl.ds(start, DH)]
+
+    def send_around(stage):
+        h, side = stage // 2, stage % 2
+        for t in range(2):
+            src = block(arrays[t][0], opposite + side, h)
+            send(src, rb.at[t, stage], xs.at[t, h], br.at[t, stage], along_seq(target + core))
+
+    def hand_on(stage):
+        h, side = stage // 2, stage % 2
+        for t in range(2):
+            wait(rb.at[t, stage], br.at[t, stage])
+            send(rb.at[t, stage], arrays[t][1].at[h, origin], bs.at[t, stage], xr.at[t, h], along_seq(target + side))
+
+    def send_stage(stage):
+        h, side = stage // 2, stage % 2
+        for t in (2, 0, 1):
+            src, dst = arrays[t]
 
             def one(step, _):
-                other = (seq // 2 + step) % 4 * 2 + core
-                start = pl.multiple_of((other * HERE + h) * DH, DH)
-                block = src.at[0, 0, :, pl.ds(start, DH)]
+                other = (chip + step) % 4 * 2 + side
 
                 @pl.when(other != seq)
                 def _():
-                    send(block, dst.at[h, seq], xs.at[t, h], xr.at[t, h], along_seq(other))
+                    send(block(src, other, h), dst.at[h, seq], xs.at[t, h], xr.at[t, h], along_seq(other))
 
                 @pl.when(other == seq)
                 def _():
-                    copy(block, dst.at[h, seq], xr.at[t, h])
+                    copy(block(src, other, h), dst.at[h, seq], xr.at[t, h])
 
                 return 0
 
-            lax.fori_loop(0, 4, one, 0)
-
-    send_head(0, 0)
-    send_head(0, 1)
+            if t == 2:
+                lax.fori_loop(1, 5, one, 0)
+            else:
+                lax.fori_loop(3, 6, one, 0)
+
+    def advance(stage):
+        hand_on(stage)
+        if stage + 1 < 2 * HERE:
+            send_stage(stage + 1)
+        if stage + 2 < 2 * HERE:
+            send_around(stage + 2)
+
+    send_around(0)
+    send_stage(0)
+    send_around(1)
 
     for i, (src, dst) in enumerate(small):
         pltpu.make_async_copy(src, dst, ins.at[i]).wait()
@@ -146,9 +177,7 @@
 
     lax.fori_loop(1, ROW, send_pack, 0)
 
-    for h in range(1, HERE):
-        send_head(h, 0)
-        send_head(h, 1)
+    advance(0)
 
     def head_sums(c, carry):
         at = pl.multiple_of(c * FEAT, FEAT)
@@ -180,7 +209,7 @@
 
         vt[...] = vb[h].reshape(SEQ * TOK, DH).T
 
-        def block(step, _):
+        def rows_block(step, _):
             j = (step + 2 * (1 - z // 4)) % 4
             rows = qb[h, pl.ds(2 * j, 2)].reshape(2 * TOK, DH)
             scores = dot(kb[h].reshape(SEQ * TOK, DH), rows, ((1,), (1,)))
@@ -203,7 +232,7 @@
 
             return 0
 
-        lax.fori_loop(0, SEQ // 2, block, 0)
+        lax.fori_loop(0, SEQ // 2, rows_block, 0)
 
     def join(u, _):
         a0, a1 = pk[u + 1, 32:33, :], pk[u + 1, 33:34, :]
@@ -237,19 +266,26 @@
             mt[w, i * TOK : (i + 1) * TOK, TOK:] = lower
         return 0
 
+    advance(1)
     attend(0)
+    advance(2)
 
     wait(pk.at[2:4], pr.at[0])
     wait(pk.at[8:10], pr.at[2])
     send(pk.at[8:10], pk.at[0:2], pys.at[0], pyr.at[0], along_view(nxt))
     send(pk.at[2:4], pk.at[10:12], pys.at[1], pyr.at[1], along_view(prv))
 
+    advance(3)
     attend(1)
+    advance(4)
     wait(pk.at[4:8], pr.at[1])
     wait(pk.at[0:2], pyr.at[0])
     wait(pk.at[10:12], pyr.at[1])
+    advance(5)
     lax.fori_loop(0, ROW + 2, join, 0)
     attend(2)
+    advance(6)
+    advance(7)
     lax.fori_loop(0, ROW, compose, 0)
     attend(3)
 
@@ -342,6 +378,9 @@
     for h in range(HERE):
         for t, (_, dst) in enumerate(arrays):
             wait(dst.at[h, 0 : SEQ - 1], xs.at[t, h])
+            if t < 2:
+                for side in range(2):
+                    wait(rb.at[t, 2 * h + side], bs.at[t, 2 * h + side])
         wait(att.at[h, 0 : ROW - 1], zs.at[h])
         wait(ext.at[h, 8:10], ys.at[h, 0])
         wait(ext.at[h, 2:4], ys.at[h, 1])
@@ -383,6 +422,7 @@
             pltpu.VMEM((HERE, SEQ) + block, BF),
             pltpu.VMEM((HERE, SEQ) + block, BF),
             pltpu.VMEM((HERE, SEQ) + block, BF),
+            pltpu.VMEM((2, 2 * HERE) + block, BF),
             pltpu.VMEM((HERE, SEQ) + block, BF),
             pltpu.VMEM((HERE, ROW + 4) + block, BF),
             pltpu.VMEM((SEQ, PACK, TOK), F32),
@@ -404,6 +444,7 @@
             pltpu.VMEM((LAT, TOK), BF),
             dma((10,)),
             dma((3, HERE)), dma((3, HERE)),
+            dma((2, 2 * HERE)), dma((2, 2 * HERE)),
             dma((HERE,)), dma((HERE, 3)),
             dma((HERE, 2)), dma((HERE, 2)),
             dma(()), dma((3,)),

time: 90.4 us -> 93.8 us (1.038)
  Pallas kernels: 88.8 us -> 92.3 us
    pallas_call x1, Pallas kernels: 88.8 us -> 92.3 us  [local(): pl.pallas_call(kernel, out_shape=jax.ShapeDtypeStruct((1, 1, LAT, TOK), F...]
where the time goes in v2:
time: 93.8 us; the launch traced here: 93.7 us
  Pallas kernels  92.3 us (98%)
  local copies, waits for them, and re-layouts  1.38 us (1%)
    pallas_call x1, Pallas kernels, local(): pl.pallas_call(kernel, out_shape=jax.ShapeDtypeStruct((1, 1, LAT, TOK), F...  92.3 us

profile of v2, /device:TPU:7, one launch (start us, length us, event | category | flops | bytes accessed | tf_op | source)
XLA Modules:
  0.0 93.7 jit_solution(3671684310450739044)
XLA Ops:
  0.0 92.3 %shard_map.127 = f32[1,1,64,128]{3,2,1,0:T(8,128)} custom-call(bf16[1,1,128,4096]{3,2,1,0:T(8,128)(2,1)} %q.1, bf16[1,1,128,4096]{3,2,1,0:T(8,128)(2,1)} %k.1, bf16[1,1,128,4096]{3,2,1,0:T(8,128)(2,1)} %v.1, s32[1,1,4,3072]{3,2,1,0:T(4,128)} %fi_in.1, f32[1,1,4,3072]{3,2,1,0:T(4,128)} %fw_in.1, s32[1,1,2,1024]{3,2,1,0:T(2,128)} %om_in.1, ...), custom_call_target="tpu_custom_call" | custom-call | tf_op jit(solution)/shard_map/pallas_call | solution.py:406
  92.3 1.4 %copy.15 = f32[1,1,64,128]{3,2,1,0:T(8,128)} copy(f32[1,1,64,128]{3,2,1,0:T(8,128)} %shard_map.127) | data formatting | bytes 65536

commit v3 on v2

--- a/solution.py
+++ b/solution.py
@@ -44,8 +44,8 @@
 def kernel(
     q, k, v, fi_in, fw_in, om_in, bi_in, bw_in, gain_in, shift_in, hw_in, lat_in, mix_in, out,
     fi, fw, om, bi, bw, gain, shift, hw, lat, mix,
-    kb, vb, qb, rb, att, ext, pks, pk, vt, jt, mt, acc, stats, wg, gsum, hsum, cols, sp, rp, vs, vsb, vown, voth,
-    ins, xs, xr, bs, br, zs, zr, ys, yr, ps, pr, pys, pyr, rs, rr, fs, fr,
+    kvq, heads, rb, att, ext, pks, pk, vt, jt, mt, acc, stats, wg, gsum, hsum, cols, sp, rp, vs, vsb, vown, voth,
+    ins, ks, xs, xr, bs, br, zs, zr, ys, yr, ps, pr, pys, pyr, rs, rr, fs, fr,
 ):
     view, eye, seq = lax.axis_index("view"), lax.axis_index("eye"), lax.axis_index("seq")
     row, z = view // ROW, view % ROW
@@ -73,6 +73,8 @@
         (fi_in, fi), (fw_in, fw), (om_in, om), (bi_in, bi), (bw_in, bw),
         (gain_in, gain), (shift_in, shift), (hw_in, hw), (lat_in, lat), (mix_in, mix),
     )
+    for t, src in enumerate((k, v, q)):
+        copy(src.at[0, 0], kvq.at[t], ks.at[t])
     for i, (src, dst) in enumerate(small):
         copy(src, dst, ins.at[i])
 
@@ -98,46 +100,34 @@
     opposite = (chip + 2) % 4 * 2
     target = (chip + 1 + 2 * core) % 4 * 2
     origin = (chip + 3 - 2 * core) % 4 * 2 + core
-    arrays = ((k, kb), (v, vb), (q, qb))
-
-    def block(src, other, h):
+
+    def block(other, h):
         start = pl.multiple_of((other * HERE + h) * DH, DH)
-        return src.at[0, 0, :, pl.ds(start, DH)]
+        return kvq.at[:, :, pl.ds(start, DH)]
 
     def send_around(stage):
         h, side = stage // 2, stage % 2
-        for t in range(2):
-            src = block(arrays[t][0], opposite + side, h)
-            send(src, rb.at[t, stage], xs.at[t, h], br.at[t, stage], along_seq(target + core))
+        send(block(opposite + side, h), rb.at[stage], xs.at[h], br.at[stage], along_seq(target + core))
 
     def hand_on(stage):
         h, side = stage // 2, stage % 2
-        for t in range(2):
-            wait(rb.at[t, stage], br.at[t, stage])
-            send(rb.at[t, stage], arrays[t][1].at[h, origin], bs.at[t, stage], xr.at[t, h], along_seq(target + side))
+        wait(rb.at[stage], br.at[stage])
+        send(rb.at[stage], heads.at[h, :, origin], bs.at[stage], xr.at[h], along_seq(target + side))
 
     def send_stage(stage):
         h, side = stage // 2, stage % 2
-        for t in (2, 0, 1):
-            src, dst = arrays[t]
-
-            def one(step, _):
-                other = (chip + step) % 4 * 2 + side
-
-                @pl.when(other != seq)
-                def _():
-                    send(block(src, other, h), dst.at[h, seq], xs.at[t, h], xr.at[t, h], along_seq(other))
-
-                @pl.when(other == seq)
-                def _():
-                    copy(block(src, other, h), dst.at[h, seq], xr.at[t, h])
-
-                return 0
-
-            if t == 2:
-                lax.fori_loop(1, 5, one, 0)
-            else:
-                lax.fori_loop(3, 6, one, 0)
+        for step in (1, 3):
+            other = (chip + step) % 4 * 2 + side
+            send(block(other, h), heads.at[h, :, seq], xs.at[h], xr.at[h], along_seq(other))
+        other = chip * 2 + side
+
+        @pl.when(core != side)
+        def _():
+            send(block(other, h), heads.at[h, :, seq], xs.at[h], xr.at[h], along_seq(other))
+
+        @pl.when(core == side)
+        def _():
+            copy(block(other, h), heads.at[h, :, seq], xr.at[h])
 
     def advance(stage):
         hand_on(stage)
@@ -146,6 +136,8 @@
         if stage + 2 < 2 * HERE:
             send_around(stage + 2)
 
+    for t in range(3):
+        wait(kvq.at[t], ks.at[t])
     send_around(0)
     send_stage(0)
     send_around(1)
@@ -204,22 +196,19 @@
     rate = math.log2(math.e) / math.sqrt(DH)
 
     def attend(h):
-        for t, (_, dst) in enumerate(arrays):
-            wait(dst.at[h], xr.at[t, h])
-
-        vt[...] = vb[h].reshape(SEQ * TOK, DH).T
+        wait(heads.at[h], xr.at[h])
+        vt[...] = heads[h, 1].reshape(SEQ * TOK, DH).T
 
         def rows_block(step, _):
-            j = (step + 2 * (1 - z // 4)) % 4
-            rows = qb[h, pl.ds(2 * j, 2)].reshape(2 * TOK, DH)
-            scores = dot(kb[h].reshape(SEQ * TOK, DH), rows, ((1,), (1,)))
+            groups = [(z + 1 + 2 * step + half) % SEQ for half in range(2)]
+            rows = jnp.concatenate([heads[h, 2, g] for g in groups], axis=0)
+            scores = dot(heads[h, 0].reshape(SEQ * TOK, DH), rows, ((1,), (1,)))
             highest = jnp.max(scores, axis=0, keepdims=True)
             probs = jnp.exp2((scores - highest) * rate)
             total = jnp.sum(probs, axis=0, keepdims=True)
             mixed = dot(vt[...], probs.astype(BF), ((1,), (0,)))
             mixed = (mixed / total).astype(BF)
-            for half in range(2):
-                g = 2 * j + half
+            for half, g in enumerate(groups):
                 att[h, g] = mixed[:, half * TOK : (half + 1) * TOK]
 
                 @pl.when(g != z)
@@ -376,11 +365,9 @@
     out[0, 0] = lat[0, 0] - 0.8 * (mine + cols[1] * (voth[...].astype(F32) - mine))
 
     for h in range(HERE):
-        for t, (_, dst) in enumerate(arrays):
-            wait(dst.at[h, 0 : SEQ - 1], xs.at[t, h])
-            if t < 2:
-                for side in range(2):
-                    wait(rb.at[t, 2 * h + side], bs.at[t, 2 * h + side])
+        wait(heads.at[h, :, 0 : SEQ - 1], xs.at[h])
+        for side in range(2):
+            wait(rb.at[2 * h + side], bs.at[2 * h + side])
         wait(att.at[h, 0 : ROW - 1], zs.at[h])
         wait(ext.at[h, 8:10], ys.at[h, 0])
         wait(ext.at[h, 2:4], ys.at[h, 1])
@@ -419,10 +406,9 @@
             pltpu.VMEM((LAT, SEQ * FEAT), BF),
             pltpu.VMEM((1, 1, LAT, TOK), F32),
             pltpu.VMEM((1, LAT), F32),
-            pltpu.VMEM((HERE, SEQ) + block, BF),
-            pltpu.VMEM((HERE, SEQ) + block, BF),
-            pltpu.VMEM((HERE, SEQ) + block, BF),
-            pltpu.VMEM((2, 2 * HERE) + block, BF),
+            pltpu.VMEM((3, TOK, SEQ * FEAT), BF),
+            pltpu.VMEM((HERE, 3, SEQ) + block, BF),
+            pltpu.VMEM((2 * HERE, 3) + block, BF),
             pltpu.VMEM((HERE, SEQ) + block, BF),
             pltpu.VMEM((HERE, ROW + 4) + block, BF),
             pltpu.VMEM((SEQ, PACK, TOK), F32),
@@ -443,8 +429,9 @@
             pltpu.VMEM((LAT, TOK), F32),
             pltpu.VMEM((LAT, TOK), BF),
             dma((10,)),
-            dma((3, HERE)), dma((3, HERE)),
-            dma((2, 2 * HERE)), dma((2, 2 * HERE)),
+            dma((3,)),
+            dma((HERE,)), dma((HERE,)),
+            dma((2 * HERE,)), dma((2 * HERE,)),
             dma((HERE,)), dma((HERE, 3)),
             dma((HERE, 2)), dma((HERE, 2)),
             dma(()), dma((3,)),

time: 93.8 us -> 92.8 us (0.989)
  Pallas kernels: 92.3 us -> 91.1 us
    pallas_call x1, Pallas kernels: 92.3 us -> 91.1 us  [local(): pl.pallas_call(kernel, out_shape=jax.ShapeDtypeStruct((1, 1, LAT, TOK), F...]
where the time goes in v3:
time: 92.8 us; the launch traced here: 92.5 us
  Pallas kernels  91.1 us (98%)
  local copies, waits for them, and re-layouts  1.38 us (1%)
    pallas_call x1, Pallas kernels, local(): pl.pallas_call(kernel, out_shape=jax.ShapeDtypeStruct((1, 1, LAT, TOK), F...  91.1 us

profile of v3, /device:TPU:7, one launch (start us, length us, event | category | flops | bytes accessed | tf_op | source)
XLA Modules:
  0.0 92.5 jit_solution(2090003521519680138)
XLA Ops:
  0.0 91.1 %shard_map.127 = f32[1,1,64,128]{3,2,1,0:T(8,128)} custom-call(bf16[1,1,128,4096]{3,2,1,0:T(8,128)(2,1)} %q.1, bf16[1,1,128,4096]{3,2,1,0:T(8,128)(2,1)} %k.1, bf16[1,1,128,4096]{3,2,1,0:T(8,128)(2,1)} %v.1, s32[1,1,4,3072]{3,2,1,0:T(4,128)} %fi_in.1, f32[1,1,4,3072]{3,2,1,0:T(4,128)} %fw_in.1, s32[1,1,2,1024]{3,2,1,0:T(2,128)} %om_in.1, ...), custom_call_target="tpu_custom_call" | custom-call | tf_op jit(solution)/shard_map/pallas_call | solution.py:393
  91.1 1.4 %copy.15 = f32[1,1,64,128]{3,2,1,0:T(8,128)} copy(f32[1,1,64,128]{3,2,1,0:T(8,128)} %shard_map.127) | data formatting | bytes 65536

commit v4 on v3

--- a/solution.py
+++ b/solution.py
@@ -199,31 +199,35 @@
         wait(heads.at[h], xr.at[h])
         vt[...] = heads[h, 1].reshape(SEQ * TOK, DH).T
 
-        def rows_block(step, _):
-            groups = [(z + 1 + 2 * step + half) % SEQ for half in range(2)]
-            rows = jnp.concatenate([heads[h, 2, g] for g in groups], axis=0)
-            scores = dot(heads[h, 0].reshape(SEQ * TOK, DH), rows, ((1,), (1,)))
-            highest = jnp.max(scores, axis=0, keepdims=True)
-            probs = jnp.exp2((scores - highest) * rate)
-            total = jnp.sum(probs, axis=0, keepdims=True)
-            mixed = dot(vt[...], probs.astype(BF), ((1,), (0,)))
-            mixed = (mixed / total).astype(BF)
-            for half, g in enumerate(groups):
-                att[h, g] = mixed[:, half * TOK : (half + 1) * TOK]
-
-                @pl.when(g != z)
-                def _():
-                    send(att.at[h, g], ext.at[h, 2 + z], zs.at[h], zr.at[h, edge], along_view(first + g))
-
-                @pl.when(g == z)
-                def _():
-                    copy(att.at[h, g], ext.at[h, 2 + z], zr.at[h, edge])
+        def query_blocks(step, _):
+            groups = [(z + 1 + 4 * step + i) % SEQ for i in range(4)]
+            keyed = heads[h, 0].reshape(SEQ * TOK, DH)
+            rows = [jnp.concatenate([heads[h, 2, g] for g in groups[i : i + 2]], axis=0) for i in (0, 2)]
+            scores = [dot(keyed, r, ((1,), (1,))) for r in rows]
+            highest = [jnp.max(x, axis=0, keepdims=True) for x in scores]
+            probs = [jnp.exp2((x - m) * rate) for x, m in zip(scores, highest)]
+            total = [jnp.sum(p, axis=0, keepdims=True) for p in probs]
+            mixed = [dot(vt[...], p.astype(BF), ((1,), (0,))) for p in probs]
+            mixed = [(m / t).astype(BF) for m, t in zip(mixed, total)]
+            for i, g in enumerate(groups):
+                att[h, g] = mixed[i // 2][:, i % 2 * TOK : (i % 2 + 1) * TOK]
+            for g in groups[:3]:
+                send(att.at[h, g], ext.at[h, 2 + z], zs.at[h], zr.at[h, edge], along_view(first + g))
+            g = groups[3]
+
+            @pl.when(step == 0)
+            def _():
+                send(att.at[h, g], ext.at[h, 2 + z], zs.at[h], zr.at[h, edge], along_view(first + g))
+
+            @pl.when(step == 1)
+            def _():
+                copy(att.at[h, g], ext.at[h, 2 + z], zr.at[h, edge])
 
             return 0
 
-        lax.fori_loop(0, SEQ // 2, rows_block, 0)
-
-    def join(u, _):
+        lax.fori_loop(0, 2, query_blocks, 0)
+
+    def join(u):
         a0, a1 = pk[u + 1, 32:33, :], pk[u + 1, 33:34, :]
         share = 1.0 / (1.0 + a0 + a1)
         for i, factor in enumerate((a0 * share, share, a1 * share)):
@@ -236,10 +240,9 @@
             upper, lower = split(part)
             jt[u, i * TOK : (i + 1) * TOK, :] = upper
             jt[u, (3 + i) * TOK : (4 + i) * TOK, :] = lower
-        return 0
-
-
-    def compose(w, _):
+
+
+    def compose(w):
         back = spread(pk[w + 2, 24:28, :], pk[w + 2, 28:32, :], 3 * TOK)
         parts = [jnp.zeros((TOK, TOK), F32) for _ in range(5)]
         for b in range(3):
@@ -253,7 +256,75 @@
             upper, lower = split(parts[i])
             mt[w, i * TOK : (i + 1) * TOK, :TOK] = upper
             mt[w, i * TOK : (i + 1) * TOK, TOK:] = lower
-        return 0
+
+    def in_pairs(count, step):
+        def two(i, _):
+            step(2 * i)
+            step(2 * i + 1)
+            return 0
+
+        lax.fori_loop(0, count // 2, two, 0)
+
+    def blend(h, views):
+        wide = [
+            dot(jnp.concatenate([ext[h, w + i] for i in range(5)], axis=1), mt[w], ((1,), (0,)))
+            for w in views
+        ]
+        x = [a[:, :TOK] + a[:, TOK:] for a in wide]
+        mean = [jnp.sum(a, axis=0, keepdims=True) * (1.0 / DH) for a in x]
+        centred = [a - m for a, m in zip(x, mean)]
+        squares = [jnp.sum(a * a, axis=0, keepdims=True) for a in centred]
+        wide = dot(wg[h], jnp.concatenate([a.astype(BF) for a in centred], axis=1), ((1,), (0,)))
+        wide = wide[:LAT] + wide[LAT:]
+        part = [wide[:, i * TOK : (i + 1) * TOK] for i in range(len(views))]
+        if h > 0:
+            part = [a + acc[w] for a, w in zip(part, views)]
+        for a, m, w in zip(squares, mean, views):
+            stats[w, h : h + 1, :] = m
+            stats[w, HERE + h : HERE + h + 1, :] = a
+        if h < HERE - 1:
+            for a, w in zip(part, views):
+                acc[w] = a
+            return
+
+        for part_here, w in zip(part, views):
+            means = stats[w, 0:HERE, :]
+            middle = jnp.sum(means, axis=0, keepdims=True) * (1.0 / HERE)
+            apart = means - middle
+            summed = jnp.sum(stats[w, HERE:, :] + DH * apart * apart, axis=0, keepdims=True)
+            for i in range(HERE):
+                part_here = part_here + hsum[i] * apart[i : i + 1]
+            rows = []
+            for line in (middle, summed):
+                for _ in range(3):
+                    piece = line.astype(BF).astype(F32)
+                    rows.append(piece)
+                    line = line - piece
+            rows.append(jnp.zeros((10, TOK), F32))
+            sp[w, 0:LAT, :] = part_here.astype(BF)
+            sp[w, LAT:, :] = jnp.concatenate(rows, axis=0).astype(BF)
+        for w in views:
+
+            @pl.when(w != seq)
+            def _():
+                send(sp.at[w], rp.at[seq], rs, rr, along_seq(w))
+
+            @pl.when(w == seq)
+            def _():
+                copy(sp.at[w], rp.at[seq], rr)
+
+    def forward(h):
+        wait(ext.at[h, 2:4], zr.at[h, 0])
+        wait(ext.at[h, 8:10], zr.at[h, 2])
+        send(ext.at[h, 8:10], ext.at[h, 0:2], ys.at[h, 0], yr.at[h, 0], along_view(nxt))
+        send(ext.at[h, 2:4], ext.at[h, 10:12], ys.at[h, 1], yr.at[h, 1], along_view(prv))
+
+    def finish(h):
+        wait(ext.at[h, 4:8], zr.at[h, 1])
+        blend(h, (2, 3, 4, 5))
+        wait(ext.at[h, 0:2], yr.at[h, 0])
+        wait(ext.at[h, 10:12], yr.at[h, 1])
+        blend(h, (0, 1, 6, 7))
 
     advance(1)
     attend(0)
@@ -271,70 +342,20 @@
     wait(pk.at[0:2], pyr.at[0])
     wait(pk.at[10:12], pyr.at[1])
     advance(5)
-    lax.fori_loop(0, ROW + 2, join, 0)
+    in_pairs(ROW + 2, join)
     attend(2)
     advance(6)
     advance(7)
-    lax.fori_loop(0, ROW, compose, 0)
+    in_pairs(ROW, compose)
+    forward(0)
+    finish(0)
+    forward(1)
     attend(3)
-
-    def blend(h, low, high):
-        def one(w, _):
-            source = jnp.concatenate([ext[h, w + i] for i in range(5)], axis=1)
-            wide = dot(source, mt[w], ((1,), (0,)))
-            x = wide[:, :TOK] + wide[:, TOK:]
-            mean = jnp.sum(x, axis=0, keepdims=True) * (1.0 / DH)
-            centred = x - mean
-            stats[w, h : h + 1, :] = mean
-            stats[w, HERE + h : HERE + h + 1, :] = jnp.sum(centred * centred, axis=0, keepdims=True)
-            wide = dot(wg[h], centred.astype(BF), ((1,), (0,)))
-            part = wide[:LAT] + wide[LAT:]
-            if h > 0:
-                part = part + acc[w]
-            if h < HERE - 1:
-                acc[w] = part
-                return 0
-
-            means = stats[w, 0:HERE, :]
-            mean = jnp.sum(means, axis=0, keepdims=True) * (1.0 / HERE)
-            apart = means - mean
-            squares = jnp.sum(stats[w, HERE:, :] + DH * apart * apart, axis=0, keepdims=True)
-            for i in range(HERE):
-                part = part + hsum[i] * apart[i : i + 1]
-            rows = []
-            for row in (mean, squares):
-                for _ in range(3):
-                    piece = row.astype(BF).astype(F32)
-                    rows.append(piece)
-                    row = row - piece
-            rows.append(jnp.zeros((10, TOK), F32))
-            sp[w, 0:LAT, :] = part.astype(BF)
-            sp[w, LAT:, :] = jnp.concatenate(rows, axis=0).astype(BF)
-
-            @pl.when(w != seq)
-            def _():
-                send(sp.at[w], rp.at[seq], rs, rr, along_seq(w))
-
-            @pl.when(w == seq)
-            def _():
-                copy(sp.at[w], rp.at[seq], rr)
-
-            return 0
-
-        lax.fori_loop(low, high, one, 0)
-
-    for h in range(HERE):
-        wait(ext.at[h, 2:4], zr.at[h, 0])
-        wait(ext.at[h, 8:10], zr.at[h, 2])
-        send(ext.at[h, 8:10], ext.at[h, 0:2], ys.at[h, 0], yr.at[h, 0], along_view(nxt))
-        send(ext.at[h, 2:4], ext.at[h, 10:12], ys.at[h, 1], yr.at[h, 1], along_view(prv))
-        wait(ext.at[h, 4:8], zr.at[h, 1])
-        blend(h, 2, 6)
-        wait(ext.at[h, 0:2], yr.at[h, 0])
-        blend(h, 0, 2)
-        wait(ext.at[h, 10:12], yr.at[h, 1])
-        blend(h, 6, 8)
-
+    forward(2)
+    finish(1)
+    finish(2)
+    forward(3)
+    finish(3)
     wait(rp, rr)
     pieces = rp[:, LAT:, :].astype(F32)
     means = pieces[:, 0] + pieces[:, 1] + pieces[:, 2]

time: 92.8 us -> 90.6 us (0.976)
  Pallas kernels: 91.1 us -> 89 us
    pallas_call x1, Pallas kernels: 91.1 us -> 89 us  [local(): pl.pallas_call(kernel, out_shape=jax.ShapeDtypeStruct((1, 1, LAT, TOK), F...]
where the time goes in v4:
time: 90.6 us; the launch traced here: 90.4 us
  Pallas kernels  89 us (98%)
  local copies, waits for them, and re-layouts  1.38 us (2%)
    pallas_call x1, Pallas kernels, local(): pl.pallas_call(kernel, out_shape=jax.ShapeDtypeStruct((1, 1, LAT, TOK), F...  89 us

profile of v4, /device:TPU:7, one launch (start us, length us, event | category | flops | bytes accessed | tf_op | source)
XLA Modules:
  0.0 90.4 jit_solution(13643414345192188683)
XLA Ops:
  0.0 89.0 %shard_map.127 = f32[1,1,64,128]{3,2,1,0:T(8,128)} custom-call(bf16[1,1,128,4096]{3,2,1,0:T(8,128)(2,1)} %q.1, bf16[1,1,128,4096]{3,2,1,0:T(8,128)(2,1)} %k.1, bf16[1,1,128,4096]{3,2,1,0:T(8,128)(2,1)} %v.1, s32[1,1,4,3072]{3,2,1,0:T(4,128)} %fi_in.1, f32[1,1,4,3072]{3,2,1,0:T(4,128)} %fw_in.1, s32[1,1,2,1024]{3,2,1,0:T(2,128)} %om_in.1, ...), custom_call_target="tpu_custom_call" | custom-call | tf_op jit(solution)/shard_map/pallas_call | solution.py:414
  89.0 1.4 %copy.15 = f32[1,1,64,128]{3,2,1,0:T(8,128)} copy(f32[1,1,64,128]{3,2,1,0:T(8,128)} %shard_map.127) | data formatting | bytes 65536

commit v5 on v4

--- a/solution.py
+++ b/solution.py
@@ -44,8 +44,8 @@
 def kernel(
     q, k, v, fi_in, fw_in, om_in, bi_in, bw_in, gain_in, shift_in, hw_in, lat_in, mix_in, out,
     fi, fw, om, bi, bw, gain, shift, hw, lat, mix,
-    kvq, heads, rb, att, ext, pks, pk, vt, jt, mt, acc, stats, wg, gsum, hsum, cols, sp, rp, vs, vsb, vown, voth,
-    ins, ks, xs, xr, bs, br, zs, zr, ys, yr, ps, pr, pys, pyr, rs, rr, fs, fr,
+    kvq, heads, att, ext, pks, pk, vt, jt, mt, acc, stats, wg, gsum, hsum, cols, sp, rp, vs, vsb, vown, voth,
+    ins, ks, xs, xr, zs, zr, ys, yr, ps, pr, pys, pyr, rs, rr, fs, fr,
 ):
     view, eye, seq = lax.axis_index("view"), lax.axis_index("eye"), lax.axis_index("seq")
     row, z = view // ROW, view % ROW
@@ -97,50 +97,29 @@
     pl.semaphore_wait(barrier, 2 * (SEQ - 1) + 3 + jnp.where(z == seq, 0, 1))
 
     chip, core = seq // 2, seq % 2
-    opposite = (chip + 2) % 4 * 2
-    target = (chip + 1 + 2 * core) % 4 * 2
-    origin = (chip + 3 - 2 * core) % 4 * 2 + core
-
-    def block(other, h):
-        start = pl.multiple_of((other * HERE + h) * DH, DH)
-        return kvq.at[:, :, pl.ds(start, DH)]
-
-    def send_around(stage):
-        h, side = stage // 2, stage % 2
-        send(block(opposite + side, h), rb.at[stage], xs.at[h], br.at[stage], along_seq(target + core))
-
-    def hand_on(stage):
-        h, side = stage // 2, stage % 2
-        wait(rb.at[stage], br.at[stage])
-        send(rb.at[stage], heads.at[h, :, origin], bs.at[stage], xr.at[h], along_seq(target + side))
-
-    def send_stage(stage):
-        h, side = stage // 2, stage % 2
-        for step in (1, 3):
-            other = (chip + step) % 4 * 2 + side
-            send(block(other, h), heads.at[h, :, seq], xs.at[h], xr.at[h], along_seq(other))
-        other = chip * 2 + side
-
-        @pl.when(core != side)
-        def _():
-            send(block(other, h), heads.at[h, :, seq], xs.at[h], xr.at[h], along_seq(other))
-
-        @pl.when(core == side)
-        def _():
-            copy(block(other, h), heads.at[h, :, seq], xr.at[h])
-
-    def advance(stage):
-        hand_on(stage)
-        if stage + 1 < 2 * HERE:
-            send_stage(stage + 1)
-        if stage + 2 < 2 * HERE:
-            send_around(stage + 2)
+
+    def send_head(h):
+        for side in range(2):
+            for step in (1, 3, 2, 0):
+                other = (chip + step) % 4 * 2 + side
+                start = pl.multiple_of((other * HERE + h) * DH, DH)
+                block = kvq.at[:, :, pl.ds(start, DH)]
+                if step > 0:
+                    send(block, heads.at[h, :, seq], xs.at[h], xr.at[h], along_seq(other))
+                    continue
+
+                @pl.when(core != side)
+                def _():
+                    send(block, heads.at[h, :, seq], xs.at[h], xr.at[h], along_seq(other))
+
+                @pl.when(core == side)
+                def _():
+                    copy(block, heads.at[h, :, seq], xr.at[h])
 
     for t in range(3):
         wait(kvq.at[t], ks.at[t])
-    send_around(0)
-    send_stage(0)
-    send_around(1)
+    send_head(0)
+    send_head(1)
 
     for i, (src, dst) in enumerate(small):
         pltpu.make_async_copy(src, dst, ins.at[i]).wait()
@@ -169,7 +148,8 @@
 
     lax.fori_loop(1, ROW, send_pack, 0)
 
-    advance(0)
+    send_head(2)
+    send_head(3)
 
     def head_sums(c, carry):
         at = pl.multiple_of(c * FEAT, FEAT)
@@ -326,26 +306,19 @@
         wait(ext.at[h, 10:12], yr.at[h, 1])
         blend(h, (0, 1, 6, 7))
 
-    advance(1)
     attend(0)
-    advance(2)
 
     wait(pk.at[2:4], pr.at[0])
     wait(pk.at[8:10], pr.at[2])
     send(pk.at[8:10], pk.at[0:2], pys.at[0], pyr.at[0], along_view(nxt))
     send(pk.at[2:4], pk.at[10:12], pys.at[1], pyr.at[1], along_view(prv))
 
-    advance(3)
     attend(1)
-    advance(4)
     wait(pk.at[4:8], pr.at[1])
     wait(pk.at[0:2], pyr.at[0])
     wait(pk.at[10:12], pyr.at[1])
-    advance(5)
     in_pairs(ROW + 2, join)
     attend(2)
-    advance(6)
-    advance(7)
     in_pairs(ROW, compose)
     forward(0)
     finish(0)
@@ -387,8 +360,6 @@
 
     for h in range(HERE):
         wait(heads.at[h, :, 0 : SEQ - 1], xs.at[h])
-        for side in range(2):
-            wait(rb.at[2 * h + side], bs.at[2 * h + side])
         wait(att.at[h, 0 : ROW - 1], zs.at[h])
         wait(ext.at[h, 8:10], ys.at[h, 0])
         wait(ext.at[h, 2:4], ys.at[h, 1])
@@ -429,7 +400,6 @@
             pltpu.VMEM((1, LAT), F32),
             pltpu.VMEM((3, TOK, SEQ * FEAT), BF),
             pltpu.VMEM((HERE, 3, SEQ) + block, BF),
-            pltpu.VMEM((2 * HERE, 3) + block, BF),
             pltpu.VMEM((HERE, SEQ) + block, BF),
             pltpu.VMEM((HERE, ROW + 4) + block, BF),
             pltpu.VMEM((SEQ, PACK, TOK), F32),
@@ -452,7 +422,6 @@
             dma((10,)),
             dma((3,)),
             dma((HERE,)), dma((HERE,)),
-            dma((2 * HERE,)), dma((2 * HERE,)),
             dma((HERE,)), dma((HERE, 3)),
             dma((HERE, 2)), dma((HERE, 2)),
             dma(()), dma((3,)),

time: 90.6 us -> 88.9 us (0.981)
  Pallas kernels: 89 us -> 87.3 us
    pallas_call x1, Pallas kernels: 89 us -> 87.3 us  [local(): pl.pallas_call(kernel, out_shape=jax.ShapeDtypeStruct((1, 1, LAT, TOK), F...]
where the time goes in v5:
time: 88.9 us; the launch traced here: 88.7 us
  Pallas kernels  87.3 us (98%)
  local copies, waits for them, and re-layouts  1.38 us (2%)
    pallas_call x1, Pallas kernels, local(): pl.pallas_call(kernel, out_shape=jax.ShapeDtypeStruct((1, 1, LAT, TOK), F...  87.3 us

profile of v5, /device:TPU:7, one launch (start us, length us, event | category | flops | bytes accessed | tf_op | source)
XLA Modules:
  0.0 88.7 jit_solution(14088034041064123528)
XLA Ops:
  0.0 87.3 %shard_map.127 = f32[1,1,64,128]{3,2,1,0:T(8,128)} custom-call(bf16[1,1,128,4096]{3,2,1,0:T(8,128)(2,1)} %q.1, bf16[1,1,128,4096]{3,2,1,0:T(8,128)(2,1)} %k.1, bf16[1,1,128,4096]{3,2,1,0:T(8,128)(2,1)} %v.1, s32[1,1,4,3072]{3,2,1,0:T(4,128)} %fi_in.1, f32[1,1,4,3072]{3,2,1,0:T(4,128)} %fw_in.1, s32[1,1,2,1024]{3,2,1,0:T(2,128)} %om_in.1, ...), custom_call_target="tpu_custom_call" | custom-call | tf_op jit(solution)/shard_map/pallas_call | solution.py:385
  87.3 1.4 %copy.15 = f32[1,1,64,128]{3,2,1,0:T(8,128)} copy(f32[1,1,64,128]{3,2,1,0:T(8,128)} %shard_map.127) | data formatting | bytes 65536

commit v6 on v5

--- a/solution.py
+++ b/solution.py
@@ -44,8 +44,8 @@
 def kernel(
     q, k, v, fi_in, fw_in, om_in, bi_in, bw_in, gain_in, shift_in, hw_in, lat_in, mix_in, out,
     fi, fw, om, bi, bw, gain, shift, hw, lat, mix,
-    kvq, heads, att, ext, pks, pk, vt, jt, mt, acc, stats, wg, gsum, hsum, cols, sp, rp, vs, vsb, vown, voth,
-    ins, ks, xs, xr, zs, zr, ys, yr, ps, pr, pys, pyr, rs, rr, fs, fr,
+    kvq, heads, rb, att, ext, pks, pk, vt, jt, mt, acc, stats, wg, gsum, hsum, cols, sp, rp, vs, vsb, vown, voth,
+    ins, ks, xs, xr, bs, br, zs, zr, ys, yr, ps, pr, pys, pyr, rs, rr, fs, fr,
 ):
     view, eye, seq = lax.axis_index("view"), lax.axis_index("eye"), lax.axis_index("seq")
     row, z = view // ROW, view % ROW
@@ -97,10 +97,24 @@
     pl.semaphore_wait(barrier, 2 * (SEQ - 1) + 3 + jnp.where(z == seq, 0, 1))
 
     chip, core = seq // 2, seq % 2
+    opposite = (chip + 2) % 4 * 2
+    target = (chip + 1 + 2 * core) % 4 * 2
+    origin = (chip + 3 - 2 * core) % 4 * 2 + core
+
+    def send_around(h):
+        for side in range(2):
+            start = pl.multiple_of(((opposite + side) * HERE + h) * DH, DH)
+            block = kvq.at[:, :, pl.ds(start, DH)]
+            send(block, rb.at[h - 1, side], xs.at[h], br.at[h - 1], along_seq(target + core))
+
+    def hand_on(h):
+        wait(rb.at[h - 1], br.at[h - 1])
+        for side in range(2):
+            send(rb.at[h - 1, side], heads.at[h, :, origin], bs.at[h - 1], xr.at[h], along_seq(target + side))
 
     def send_head(h):
         for side in range(2):
-            for step in (1, 3, 2, 0):
+            for step in (1, 3, 2, 0) if h == 0 else (1, 3, 0):
                 other = (chip + step) % 4 * 2 + side
                 start = pl.multiple_of((other * HERE + h) * DH, DH)
                 block = kvq.at[:, :, pl.ds(start, DH)]
@@ -119,7 +133,9 @@
     for t in range(3):
         wait(kvq.at[t], ks.at[t])
     send_head(0)
+    send_around(1)
     send_head(1)
+    send_around(2)
 
     for i, (src, dst) in enumerate(small):
         pltpu.make_async_copy(src, dst, ins.at[i]).wait()
@@ -148,8 +164,6 @@
 
     lax.fori_loop(1, ROW, send_pack, 0)
 
-    send_head(2)
-    send_head(3)
 
     def head_sums(c, carry):
         at = pl.multiple_of(c * FEAT, FEAT)
@@ -307,6 +321,9 @@
         blend(h, (0, 1, 6, 7))
 
     attend(0)
+    hand_on(1)
+    send_head(2)
+    send_around(3)
 
     wait(pk.at[2:4], pr.at[0])
     wait(pk.at[8:10], pr.at[2])
@@ -314,16 +331,19 @@
     send(pk.at[2:4], pk.at[10:12], pys.at[1], pyr.at[1], along_view(prv))
 
     attend(1)
+    hand_on(2)
+    send_head(3)
     wait(pk.at[4:8], pr.at[1])
     wait(pk.at[0:2], pyr.at[0])
     wait(pk.at[10:12], pyr.at[1])
     in_pairs(ROW + 2, join)
+    hand_on(3)
     attend(2)
-    in_pairs(ROW, compose)
     forward(0)
-    finish(0)
     forward(1)
     attend(3)
+    in_pairs(ROW, compose)
+    finish(0)
     forward(2)
     finish(1)
     finish(2)
@@ -360,6 +380,8 @@
 
     for h in range(HERE):
         wait(heads.at[h, :, 0 : SEQ - 1], xs.at[h])
+        if h > 0:
+            wait(rb.at[h - 1], bs.at[h - 1])
         wait(att.at[h, 0 : ROW - 1], zs.at[h])
         wait(ext.at[h, 8:10], ys.at[h, 0])
         wait(ext.at[h, 2:4], ys.at[h, 1])
@@ -400,6 +422,7 @@
             pltpu.VMEM((1, LAT), F32),
             pltpu.VMEM((3, TOK, SEQ * FEAT), BF),
             pltpu.VMEM((HERE, 3, SEQ) + block, BF),
+            pltpu.VMEM((HERE - 1, 2, 3) + block, BF),
             pltpu.VMEM((HERE, SEQ) + block, BF),
             pltpu.VMEM((HERE, ROW + 4) + block, BF),
             pltpu.VMEM((SEQ, PACK, TOK), F32),
@@ -422,6 +445,7 @@
             dma((10,)),
             dma((3,)),
             dma((HERE,)), dma((HERE,)),
+            dma((HERE - 1,)), dma((HERE - 1,)),
             dma((HERE,)), dma((HERE, 3)),
             dma((HERE, 2)), dma((HERE, 2)),
             dma(()), dma((3,)),

time: 88.9 us -> 91.1 us (1.025)
  Pallas kernels: 87.3 us -> 89.5 us
    pallas_call x1, Pallas kernels: 87.3 us -> 89.5 us  [local(): pl.pallas_call(kernel, out_shape=jax.ShapeDtypeStruct((1, 1, LAT, TOK), F...]
where the time goes in v6:
time: 91.1 us; the launch traced here: 90.9 us
  Pallas kernels  89.5 us (98%)
  local copies, waits for them, and re-layouts  1.38 us (2%)
    pallas_call x1, Pallas kernels, local(): pl.pallas_call(kernel, out_shape=jax.ShapeDtypeStruct((1, 1, LAT, TOK), F...  89.5 us

profile of v6, /device:TPU:7, one launch (start us, length us, event | category | flops | bytes accessed | tf_op | source)
XLA Modules:
  0.0 90.9 jit_solution(6106470751136735772)
XLA Ops:
  0.0 89.5 %shard_map.127 = f32[1,1,64,128]{3,2,1,0:T(8,128)} custom-call(bf16[1,1,128,4096]{3,2,1,0:T(8,128)(2,1)} %q.1, bf16[1,1,128,4096]{3,2,1,0:T(8,128)(2,1)} %k.1, bf16[1,1,128,4096]{3,2,1,0:T(8,128)(2,1)} %v.1, s32[1,1,4,3072]{3,2,1,0:T(4,128)} %fi_in.1, f32[1,1,4,3072]{3,2,1,0:T(4,128)} %fw_in.1, s32[1,1,2,1024]{3,2,1,0:T(2,128)} %om_in.1, ...), custom_call_target="tpu_custom_call" | custom-call | tf_op jit(solution)/shard_map/pallas_call | solution.py:407
  89.5 1.4 %copy.15 = f32[1,1,64,128]{3,2,1,0:T(8,128)} copy(f32[1,1,64,128]{3,2,1,0:T(8,128)} %shard_map.127) | data formatting | bytes 65536

commit v7 on v5

--- a/solution.py
+++ b/solution.py
@@ -44,7 +44,7 @@
 def kernel(
     q, k, v, fi_in, fw_in, om_in, bi_in, bw_in, gain_in, shift_in, hw_in, lat_in, mix_in, out,
     fi, fw, om, bi, bw, gain, shift, hw, lat, mix,
-    kvq, heads, att, ext, pks, pk, vt, jt, mt, acc, stats, wg, gsum, hsum, cols, sp, rp, vs, vsb, vown, voth,
+    kvq, heads, att, ext, pks, pk, vt, jt, mt, acc, stats, wg, gsum, hsum, cols, sp, rp, vsb, vown, voth,
     ins, ks, xs, xr, zs, zr, ys, yr, ps, pr, pys, pyr, rs, rr, fs, fr,
 ):
     view, eye, seq = lax.axis_index("view"), lax.axis_index("eye"), lax.axis_index("seq")
@@ -75,9 +75,6 @@
     )
     for t, src in enumerate((k, v, q)):
         copy(src.at[0, 0], kvq.at[t], ks.at[t])
-    for i, (src, dst) in enumerate(small):
-        copy(src, dst, ins.at[i])
-
     barrier = pltpu.get_barrier_semaphore()
 
     def greet(target):
@@ -93,6 +90,9 @@
     @pl.when(z != seq)
     def _():
         greet(partner)
+
+    for i, (src, dst) in enumerate(small):
+        copy(src, dst, ins.at[i])
 
     pl.semaphore_wait(barrier, 2 * (SEQ - 1) + 3 + jnp.where(z == seq, 0, 1))
 
@@ -294,9 +294,9 @@
                 copy(sp.at[w], rp.at[seq], rr)
 
     def forward(h):
-        wait(ext.at[h, 2:4], zr.at[h, 0])
         wait(ext.at[h, 8:10], zr.at[h, 2])
         send(ext.at[h, 8:10], ext.at[h, 0:2], ys.at[h, 0], yr.at[h, 0], along_view(nxt))
+        wait(ext.at[h, 2:4], zr.at[h, 0])
         send(ext.at[h, 2:4], ext.at[h, 10:12], ys.at[h, 1], yr.at[h, 1], along_view(prv))
 
     def finish(h):
@@ -341,22 +341,16 @@
     for i in range(SEQ):
         summed = summed + (rp[i, :LAT, :].astype(F32) + gsum[i] * apart[i : i + 1])
     velocity = summed / deviation + cols[0]
-    vs[...] = velocity
     vsb[...] = velocity.astype(BF)
     send(vsb, voth, fs.at[1], fr.at[1], across)
 
     @pl.when(z != seq)
     def _():
-        send(vs, vown, fs.at[0], fr.at[0], partner)
+        send(vsb, vown, fs.at[0], fr.at[0], partner)
 
     @pl.when(z == seq)
     def _():
-        copy(vs, vown, fr.at[0])
-
-    wait(vown, fr.at[0])
-    wait(voth, fr.at[1])
-    mine = vown[...]
-    out[0, 0] = lat[0, 0] - 0.8 * (mine + cols[1] * (voth[...].astype(F32) - mine))
+        copy(vsb, vown, fr.at[0])
 
     for h in range(HERE):
         wait(heads.at[h, :, 0 : SEQ - 1], xs.at[h])
@@ -367,11 +361,17 @@
     wait(pk.at[8:10], pys.at[0])
     wait(pk.at[2:4], pys.at[1])
     wait(sp.at[0 : SEQ - 1], rs)
+
+    wait(vown, fr.at[0])
+    wait(voth, fr.at[1])
+    mine = vown[...].astype(F32)
+    out[0, 0] = lat[0, 0] - 0.8 * (mine + cols[1] * (voth[...].astype(F32) - mine))
+
     wait(vsb, fs.at[1])
 
     @pl.when(z != seq)
     def _():
-        wait(vs, fs.at[0])
+        wait(vsb, fs.at[0])
 
 
 def local(
@@ -415,9 +415,8 @@
             pltpu.VMEM((2, LAT, TOK), F32),
             pltpu.VMEM((ROW, LAT + 16, TOK), BF),
             pltpu.VMEM((SEQ, LAT + 16, TOK), BF),
-            pltpu.VMEM((LAT, TOK), F32),
             pltpu.VMEM((LAT, TOK), BF),
-            pltpu.VMEM((LAT, TOK), F32),
+            pltpu.VMEM((LAT, TOK), BF),
             pltpu.VMEM((LAT, TOK), BF),
             dma((10,)),
             dma((3,)),

time: 88.9 us -> 88.5 us (level)
  no operation moved by 1% of the time
where the time goes in v7:
time: 88.5 us; the launch traced here: 88.3 us
  Pallas kernels  86.9 us (98%)
  local copies, waits for them, and re-layouts  1.38 us (2%)
    pallas_call x1, Pallas kernels, local(): pl.pallas_call(kernel, out_shape=jax.ShapeDtypeStruct((1, 1, LAT, TOK), F...  86.9 us

profile of v7, /device:TPU:7, one launch (start us, length us, event | category | flops | bytes accessed | tf_op | source)
XLA Modules:
  0.0 88.3 jit_solution(13854401268268523159)
XLA Ops:
  0.0 86.9 %shard_map.127 = f32[1,1,64,128]{3,2,1,0:T(8,128)} custom-call(bf16[1,1,128,4096]{3,2,1,0:T(8,128)(2,1)} %q.1, bf16[1,1,128,4096]{3,2,1,0:T(8,128)(2,1)} %k.1, bf16[1,1,128,4096]{3,2,1,0:T(8,128)(2,1)} %v.1, s32[1,1,4,3072]{3,2,1,0:T(4,128)} %fi_in.1, f32[1,1,4,3072]{3,2,1,0:T(4,128)} %fw_in.1, s32[1,1,2,1024]{3,2,1,0:T(2,128)} %om_in.1, ...), custom_call_target="tpu_custom_call" | custom-call | tf_op jit(solution)/shard_map/pallas_call | solution.py:385
  86.9 1.4 %copy.15 = f32[1,1,64,128]{3,2,1,0:T(8,128)} copy(f32[1,1,64,128]{3,2,1,0:T(8,128)} %shard_map.127) | data formatting | bytes 65536

commit v8 on v7

--- a/solution.py
+++ b/solution.py
@@ -45,7 +45,7 @@
     q, k, v, fi_in, fw_in, om_in, bi_in, bw_in, gain_in, shift_in, hw_in, lat_in, mix_in, out,
     fi, fw, om, bi, bw, gain, shift, hw, lat, mix,
     kvq, heads, att, ext, pks, pk, vt, jt, mt, acc, stats, wg, gsum, hsum, cols, sp, rp, vsb, vown, voth,
-    ins, ks, xs, xr, zs, zr, ys, yr, ps, pr, pys, pyr, rs, rr, fs, fr,
+    ins, ks, xs, xr, xq, zs, zr, ys, yr, ps, pr, pys, pyr, rs, rr, fs, fr,
 ):
     view, eye, seq = lax.axis_index("view"), lax.axis_index("eye"), lax.axis_index("seq")
     row, z = view // ROW, view % ROW
@@ -99,22 +99,26 @@
     chip, core = seq // 2, seq % 2
 
     def send_head(h):
+        last = h == HERE - 1
         for side in range(2):
-            for step in (1, 3, 2, 0):
-                other = (chip + step) % 4 * 2 + side
-                start = pl.multiple_of((other * HERE + h) * DH, DH)
-                block = kvq.at[:, :, pl.ds(start, DH)]
-                if step > 0:
-                    send(block, heads.at[h, :, seq], xs.at[h], xr.at[h], along_seq(other))
-                    continue
-
-                @pl.when(core != side)
-                def _():
-                    send(block, heads.at[h, :, seq], xs.at[h], xr.at[h], along_seq(other))
-
-                @pl.when(core == side)
-                def _():
-                    copy(block, heads.at[h, :, seq], xr.at[h])
+            for begin, count in ((0, 2), (2, 1)) if last else ((0, 3),):
+                for step in (1, 3, 2, 0):
+                    other = (chip + step) % 4 * 2 + side
+                    start = pl.multiple_of((other * HERE + h) * DH, DH)
+                    block = kvq.at[begin : begin + count, :, pl.ds(start, DH)]
+                    place = heads.at[h, begin : begin + count, seq]
+                    sem = xr.at[h] if begin == 0 else xq.at[0 if step in (1, 3) else 1]
+                    if step > 0:
+                        send(block, place, xs.at[h], sem, along_seq(other))
+                        continue
+
+                    @pl.when(core != side)
+                    def _():
+                        send(block, place, xs.at[h], sem, along_seq(other))
+
+                    @pl.when(core == side)
+                    def _():
+                        copy(block, place, sem)
 
     for t in range(3):
         wait(kvq.at[t], ks.at[t])
@@ -175,37 +179,49 @@
 
     rate = math.log2(math.e) / math.sqrt(DH)
 
+    def query_blocks(h, groups):
+        keyed = heads[h, 0].reshape(SEQ * TOK, DH)
+        rows = [jnp.concatenate([heads[h, 2, g] for g in groups[i : i + 2]], axis=0) for i in (0, 2)]
+        scores = [dot(keyed, r, ((1,), (1,))) for r in rows]
+        highest = [jnp.max(x, axis=0, keepdims=True) for x in scores]
+        probs = [jnp.exp2((x - m) * rate) for x, m in zip(scores, highest)]
+        total = [jnp.sum(p, axis=0, keepdims=True) for p in probs]
+        mixed = [dot(vt[...], p.astype(BF), ((1,), (0,))) for p in probs]
+        mixed = [(m / t).astype(BF) for m, t in zip(mixed, total)]
+        for i, g in enumerate(groups):
+            att[h, g] = mixed[i // 2][:, i % 2 * TOK : (i % 2 + 1) * TOK]
+
+    def send_group(h, g):
+        send(att.at[h, g], ext.at[h, 2 + z], zs.at[h], zr.at[h, edge], along_view(first + g))
+
+    def keep_group(h, g):
+        copy(att.at[h, g], ext.at[h, 2 + z], zr.at[h, edge])
+
     def attend(h):
         wait(heads.at[h], xr.at[h])
         vt[...] = heads[h, 1].reshape(SEQ * TOK, DH).T
 
-        def query_blocks(step, _):
+        def one(step, _):
             groups = [(z + 1 + 4 * step + i) % SEQ for i in range(4)]
-            keyed = heads[h, 0].reshape(SEQ * TOK, DH)
-            rows = [jnp.concatenate([heads[h, 2, g] for g in groups[i : i + 2]], axis=0) for i in (0, 2)]
-            scores = [dot(keyed, r, ((1,), (1,))) for r in rows]
-            highest = [jnp.max(x, axis=0, keepdims=True) for x in scores]
-            probs = [jnp.exp2((x - m) * rate) for x, m in zip(scores, highest)]
-            total = [jnp.sum(p, axis=0, keepdims=True) for p in probs]
-            mixed = [dot(vt[...], p.astype(BF), ((1,), (0,))) for p in probs]
-            mixed = [(m / t).astype(BF) for m, t in zip(mixed, total)]
-            for i, g in enumerate(groups):
-                att[h, g] = mixed[i // 2][:, i % 2 * TOK : (i % 2 + 1) * TOK]
+            query_blocks(h, groups)
             for g in groups[:3]:
-                send(att.at[h, g], ext.at[h, 2 + z], zs.at[h], zr.at[h, edge], along_view(first + g))
-            g = groups[3]
-
-            @pl.when(step == 0)
-            def _():
-                send(att.at[h, g], ext.at[h, 2 + z], zs.at[h], zr.at[h, edge], along_view(first + g))
-
-            @pl.when(step == 1)
-            def _():
-                copy(att.at[h, g], ext.at[h, 2 + z], zr.at[h, edge])
-
+                send_group(h, g)
+            pl.when(step == 0)(lambda: send_group(h, groups[3]))
+            pl.when(step == 1)(lambda: keep_group(h, groups[3]))
             return 0
 
-        lax.fori_loop(0, 2, query_blocks, 0)
+        lax.fori_loop(0, 2, one, 0)
+
+    def attend_last(h):
+        wait(heads.at[h, 0:2], xr.at[h])
+        vt[...] = heads[h, 1].reshape(SEQ * TOK, DH).T
+        for i, steps in enumerate(((1, 3), (2, 0))):
+            wait(heads.at[h, 2, 0:4], xq.at[i])
+            groups = [(chip + step) % 4 * 2 + side for step in steps for side in range(2)]
+            query_blocks(h, groups)
+            for g in groups:
+                pl.when(g != z)(lambda g=g: send_group(h, g))
+                pl.when(g == z)(lambda g=g: keep_group(h, g))
 
     def join(u):
         a0, a1 = pk[u + 1, 32:33, :], pk[u + 1, 33:34, :]
@@ -323,7 +339,7 @@
     forward(0)
     finish(0)
     forward(1)
-    attend(3)
+    attend_last(3)
     forward(2)
     finish(1)
     finish(2)
@@ -420,7 +436,7 @@
             pltpu.VMEM((LAT, TOK), BF),
             dma((10,)),
             dma((3,)),
-            dma((HERE,)), dma((HERE,)),
+            dma((HERE,)), dma((HERE,)), dma((2,)),
             dma((HERE,)), dma((HERE, 3)),
             dma((HERE, 2)), dma((HERE, 2)),
             dma(()), dma((3,)),

time: 88.5 us -> 88.5 us (level)
  no operation moved by 1% of the time
where the time goes in v8:
time: 88.5 us; the launch traced here: 88.3 us
  Pallas kernels  86.9 us (98%)
  local copies, waits for them, and re-layouts  1.38 us (2%)
    pallas_call x1, Pallas kernels, local(): pl.pallas_call(kernel, out_shape=jax.ShapeDtypeStruct((1, 1, LAT, TOK), F...  86.9 us

profile of v8, /device:TPU:7, one launch (start us, length us, event | category | flops | bytes accessed | tf_op | source)
XLA Modules:
  0.0 88.3 jit_solution(799564567416722687)
XLA Ops:
  0.0 86.9 %shard_map.127 = f32[1,1,64,128]{3,2,1,0:T(8,128)} custom-call(bf16[1,1,128,4096]{3,2,1,0:T(8,128)(2,1)} %q.1, bf16[1,1,128,4096]{3,2,1,0:T(8,128)(2,1)} %k.1, bf16[1,1,128,4096]{3,2,1,0:T(8,128)(2,1)} %v.1, s32[1,1,4,3072]{3,2,1,0:T(4,128)} %fi_in.1, f32[1,1,4,3072]{3,2,1,0:T(4,128)} %fw_in.1, s32[1,1,2,1024]{3,2,1,0:T(2,128)} %om_in.1, ...), custom_call_target="tpu_custom_call" | custom-call | tf_op jit(solution)/shard_map/pallas_call | solution.py:401
  86.9 1.4 %copy.15 = f32[1,1,64,128]{3,2,1,0:T(8,128)} copy(f32[1,1,64,128]{3,2,1,0:T(8,128)} %shard_map.127) | data formatting | bytes 65536

commit v9 on v8

--- a/solution.py
+++ b/solution.py
@@ -152,8 +152,6 @@
 
     lax.fori_loop(1, ROW, send_pack, 0)
 
-    send_head(2)
-    send_head(3)
 
     def head_sums(c, carry):
         at = pl.multiple_of(c * FEAT, FEAT)
@@ -323,6 +321,7 @@
         blend(h, (0, 1, 6, 7))
 
     attend(0)
+    send_head(2)
 
     wait(pk.at[2:4], pr.at[0])
     wait(pk.at[8:10], pr.at[2])
@@ -330,6 +329,7 @@
     send(pk.at[2:4], pk.at[10:12], pys.at[1], pyr.at[1], along_view(prv))
 
     attend(1)
+    send_head(3)
     wait(pk.at[4:8], pr.at[1])
     wait(pk.at[0:2], pyr.at[0])
     wait(pk.at[10:12], pyr.at[1])

time: 88.5 us -> 88.5 us (level)
  no operation moved by 1% of the time
where the time goes in v9:
time: 88.5 us; the launch traced here: 88.3 us
  Pallas kernels  86.9 us (98%)
  local copies, waits for them, and re-layouts  1.38 us (2%)
    pallas_call x1, Pallas kernels, local(): pl.pallas_call(kernel, out_shape=jax.ShapeDtypeStruct((1, 1, LAT, TOK), F...  86.9 us

profile of v9, /device:TPU:7, one launch (start us, length us, event | category | flops | bytes accessed | tf_op | source)
XLA Modules:
  0.0 88.3 jit_solution(11702825861407594428)
XLA Ops:
  0.0 86.9 %shard_map.127 = f32[1,1,64,128]{3,2,1,0:T(8,128)} custom-call(bf16[1,1,128,4096]{3,2,1,0:T(8,128)(2,1)} %q.1, bf16[1,1,128,4096]{3,2,1,0:T(8,128)(2,1)} %k.1, bf16[1,1,128,4096]{3,2,1,0:T(8,128)(2,1)} %v.1, s32[1,1,4,3072]{3,2,1,0:T(4,128)} %fi_in.1, f32[1,1,4,3072]{3,2,1,0:T(4,128)} %fw_in.1, s32[1,1,2,1024]{3,2,1,0:T(2,128)} %om_in.1, ...), custom_call_target="tpu_custom_call" | custom-call | tf_op jit(solution)/shard_map/pallas_call | solution.py:401
  86.9 1.4 %copy.15 = f32[1,1,64,128]{3,2,1,0:T(8,128)} copy(f32[1,1,64,128]{3,2,1,0:T(8,128)} %shard_map.127) | data formatting | bytes 65536
